TPU v7x, 512 devices: a whole 4x4x16 slice. The times are simulated.
512 devices in a mesh: dp: 4 (over z_hi), tm: 64 (over x, y, z_lo), space: 2 (over core).
Axes of the slice: x: 4, y: 4, z: 16 (z_hi: 4, z_lo: 4; z = z_hi * 4 + z_lo), core: 2. Of those that a mesh axis runs over, the one named last changes fastest.
Arguments:
- inputs: bfloat16 [4, 128, 16, 32, 128], P('dp', 'tm', 'space'), may hold values from -6 to 6
- clip_lengths: int32 [4, 4], P('dp'), may hold values from 1 to 64, 128 in all within a row
- weight: bfloat16 [3, 3, 3, 128, 128], replicated, may hold values from -0.109375 to 0.109375
- bias: float32 [128], replicated, may hold values from -3 to 3
- cotangent: bfloat16 [4, 128, 16, 32, 128], P('dp', 'tm', 'space'), may hold values from -6 to 6
Outputs:
- outputs: bfloat16 [4, 128, 16, 32, 128], P('dp', 'tm', 'space')
- input_grad: bfloat16 [4, 128, 16, 32, 128], P('dp', 'tm', 'space')
- weight_grad: float32 [3, 3, 3, 128, 128], replicated
- bias_grad: float32 [128], replicated
Inputs may be any that keep to these rules, and one draw needn't show every extreme that they name: `clip_lengths`: each row sums to 128 and its largest entry is exactly 64.
All inputs are finite; a program needn't handle non-finite values.
Results may differ from a plain program's by a relative error of at most 0.008.
Values may be sent and summed in bfloat16 or wider, within the bound.
A program may use at most 64 MiB of HBM per device.

v0:
```python
import jax
import jax.numpy as jnp
from jax import lax
from jax.sharding import PartitionSpec as P


def with_halo(cells, sides, width):
    for axis, dim in sides:
        count = lax.axis_size(axis)
        ends = count - 1
        head = lax.slice_in_dim(cells, 0, width, axis=dim)
        tail = lax.slice_in_dim(cells, cells.shape[dim] - width, cells.shape[dim], axis=dim)
        cells = jnp.concatenate(
            [
                lax.ppermute(tail, axis, [(i, (i + 1) % count) for i in range(ends)]),
                cells,
                lax.ppermute(head, axis, [((i + 1) % count, i) for i in range(ends)]),
            ],
            axis=dim,
        )
    return cells


def from_behind(block, axis, distance):
    devices = range(lax.axis_size(axis))
    route = [(i - distance, i) for i in devices if i - distance in devices]
    return lax.ppermute(block, axis, route)


def clip_index(lengths, frames):
    ends = jnp.cumsum(lengths)
    return jnp.sum((frames[:, None] >= ends[None, :]).astype(jnp.int32), axis=1)


def tap_masks(lengths, frames):
    own = clip_index(lengths, frames)
    rows = []
    for k in range(3):
        earlier = frames - (2 - k)
        keep = (earlier >= 0) & (clip_index(lengths, earlier) == own)
        rows.append(keep.astype(jnp.float32))
    return jnp.stack(rows)


def extend_rows(values):
    framed = with_halo(values, (("space", 1),), 1)
    return jnp.pad(framed, ((0, 0), (0, 0), (1, 1), (0, 0)))


def spread(padded, masks, weight, count, rows, cols):
    chan = weight.shape[3]
    total = jnp.zeros((count * rows * cols, chan), jnp.float32)
    for k in range(3):
        masked = padded * masks[k][:, None, None, None].astype(jnp.bfloat16)
        for above in range(3):
            for left in range(3):
                piece = masked[
                    2 - k : 2 - k + count, 2 - above : 2 - above + rows, 2 - left : 2 - left + cols
                ]
                total = total + lax.dot_general(
                    piece.reshape(-1, chan),
                    weight[k, above, left],
                    (((1,), (1,)), ((), ())),
                    preferred_element_type=jnp.float32,
                )
    return total.reshape(count, rows, cols, chan)


def on_device(inputs, clip_lengths, weight, bias, cotangent):
    local = inputs[0]
    frames_dev, rows, cols, chan = local.shape
    lengths = clip_lengths[0]
    base = lax.axis_index("tm") * frames_dev
    earlier = from_behind(local, "tm", 1)
    padded = extend_rows(jnp.concatenate([earlier, local], axis=0))
    masks = tap_masks(lengths, base + jnp.arange(frames_dev, dtype=jnp.int32))
    z = jnp.zeros((frames_dev, rows, cols, chan), jnp.float32)
    for k in range(3):
        part = jnp.zeros((frames_dev * rows * cols, chan), jnp.float32)
        for above in range(3):
            for left in range(3):
                piece = padded[
                    k : k + frames_dev, above : above + rows, left : left + cols
                ].reshape(-1, chan)
                part = part + jnp.dot(
                    piece, weight[k, above, left], preferred_element_type=jnp.float32
                )
        z = z + masks[k][:, None, None, None] * part.reshape(frames_dev, rows, cols, chan)
    z = z + bias
    sig = jax.nn.sigmoid(z)
    result = (z * sig).astype(jnp.bfloat16)
    dz = (cotangent[0].astype(jnp.float32) * sig * (1.0 + z * (1.0 - sig))).astype(jnp.bfloat16)
    kernel_rows = []
    for k in range(3):
        masked = (dz * masks[k][:, None, None, None].astype(jnp.bfloat16)).reshape(-1, chan)
        tap_rows = []
        for above in range(3):
            tap_cols = []
            for left in range(3):
                piece = padded[
                    k : k + frames_dev, above : above + rows, left : left + cols
                ].reshape(-1, chan)
                tap_cols.append(
                    lax.dot_general(
                        piece, masked, (((0,), (0,)), ((), ())), preferred_element_type=jnp.float32
                    )
                )
            tap_rows.append(jnp.stack(tap_cols))
        kernel_rows.append(jnp.stack(tap_rows))
    kern_grad = jnp.stack(kernel_rows)
    bias_terms = jnp.sum(dz.astype(jnp.float32), axis=(0, 1, 2))
    later = from_behind(dz, "tm", -1)
    stretched = extend_rows(jnp.concatenate([dz, later], axis=0))
    wide_masks = tap_masks(lengths, base + jnp.arange(frames_dev + 2, dtype=jnp.int32))
    in_grad = spread(stretched, wide_masks, weight, frames_dev, rows, cols)
    kern_total, bias_total = lax.psum((kern_grad, bias_terms), ("dp", "tm", "space"))
    return (result[None], in_grad.astype(jnp.bfloat16)[None], kern_total, bias_total)


def solution(mesh):
    return jax.shard_map(
        on_device,
        mesh=mesh,
        in_specs=(
            P("dp", "tm", "space", None, None),
            P("dp", None),
            P(),
            P(),
            P("dp", "tm", "space", None, None),
        ),
        out_specs=(
            P("dp", "tm", "space", None, None),
            P("dp", "tm", "space", None, None),
            P(),
            P(),
        ),
        check_vma=False,
    )
```

profile of v0, /device:TPU:1, one launch (start us, length us, event | category | flops | bytes accessed | tf_op | source)
XLA Modules:
  0.0 537.3 jit_solution(1012772034537038152)
XLA Ops:
  7.2 4.4 collective-permute-start
  11.7 0.8 reduce-window.8
  12.5 0.2 fusion.133
  12.7 0.2 convert_reduce_fusion.1
  13.0 0.9 collective-permute-done
  13.8 0.7 pad_maximum_fusion.6
  14.6 1.3 collective-permute-start.1
  15.9 6.3 %collective-permute-start.2 = (bf16[4,1,32,128]{3,2,1,0:T(8,128)(2,1)S(1)}, bf16[4,1,32,128]{3,2,1,0:T(8,128)(2,1)S(1)}, u32[]{:S(2)}, u32[]{:S(2)}) collective-permute-start(bf16[4,1,32,128]{3,2,1,0:T(8,128)(2,1)S(1)} %get-tuple-element.77), channel_id=1, source_target_pairs={{1,0},{3,2},{5,4},{7,6},{9,8},{11,10},{13,12},{15,14},{17,16},{19,... | collective-permute-start | bytes 98312 | tf_op jit(solution)/shard_map/ppermute | solution.py:17
  22.2 0.9 pad_maximum_fusion.2
  23.0 1.1 select_maximum_fusion.3
  24.1 0.4 fusion.167
  24.5 0.8 copy-done
  30.3 0.2 convert_reduce_fusion
  30.6 0.2 convolution_bitcast_fusion.18
  30.8 0.2 convolution_bitcast_fusion.19
  31.1 0.2 convolution_bitcast_fusion.15
  31.3 0.2 convolution_bitcast_fusion.17
  31.6 0.2 convolution_bitcast_fusion.13
  31.8 0.2 convolution_bitcast_fusion.14
  32.1 0.2 convolution_bitcast_fusion.11
  32.3 0.2 convolution_bitcast_fusion.12
  32.6 0.2 convolution_bitcast_fusion.10
  32.8 0.2 convolution_bitcast_fusion.9
  33.1 0.2 convolution_bitcast_fusion.7
  33.3 0.2 convolution_bitcast_fusion.8
  33.6 0.2 convolution_bitcast_fusion.5
  33.8 0.2 convolution_bitcast_fusion.6
  34.1 0.2 convolution_bitcast_fusion.2
  34.4 0.2 convolution_bitcast_fusion.4
  34.6 0.2 convolution_bitcast_fusion
  34.9 0.2 convolution_bitcast_fusion.1
  35.1 1.3 collective-permute-start.3
  36.4 0.8 multiply_convert_fusion
  37.2 0.3 convolution_bitcast_fusion.3
  37.5 0.2 convolution_bitcast_fusion.26
  37.8 0.2 convolution_bitcast_fusion.16
  38.1 0.2 convolution_bitcast_fusion.25
  38.4 0.2 convolution_bitcast_fusion.24
  38.7 0.2 convolution_bitcast_fusion.23
  39.0 0.2 convolution_bitcast_fusion.22
  39.3 0.2 convolution_bitcast_fusion.21
  39.6 0.2 convolution_bitcast_fusion.20
  39.9 2.8 collective-permute-done.3
  42.8 1.3 collective-permute-start.4
  44.1 3.0 collective-permute-start.5
  47.1 1.4 pad_maximum_fusion
  48.5 112.2 %psum.15 = f32[128]{0:T(128)} all-reduce(f32[128]{0:T(128)S(1)} %get-tuple-element.10), channel_id=1, replica_groups=mesh['dp'=4,'tm'=64,'space'=2] {'dp','tm','space'}, use_global_device_ids=true, to_apply=%region_9.10 | all-reduce | flops 128 | bytes 1024 | tf_op jit(solution)/shard_map/psum | solution.py:116
  160.7 0.3 broadcast_multiply_fusion
  161.9 0.2 convolution_add_fusion.24
  162.1 0.2 convolution_add_fusion.23
  162.5 0.2 convolution_add_fusion.21
  162.7 0.2 convolution_add_fusion.20
  162.9 0.2 convolution_add_fusion.19
  163.1 0.2 convolution_add_fusion.18
  163.3 0.2 convolution_add_fusion.17
  163.9 0.2 convolution_add_fusion.14
  164.3 0.2 convolution_add_fusion.12
  164.6 0.2 convolution_add_fusion.10
  165.2 0.2 convolution_add_fusion.7
  165.6 0.2 convolution_add_fusion.5
  166.0 0.2 convolution_add_fusion.3
  166.6 0.8 fusion.2
  167.4 360.2 %all-reduce.4.cloned.1.call-done = f32[3,3,3,128,128]{4,3,2,1,0:T(8,128)} async-done(((f32[3,3,3,128,128]{4,3,2,1,0:T(8,128)}), f32[3,3,3,128,128]{4,3,2,1,0:T(8,128)}) %all-reduce.4.cloned.1.call-update) | async-done | bytes 1769488 | tf_op jit(solution)/shard_map/psum | solution.py:116
  527.6 2.9 copy.43
  (80 shorter events, 8.1 us)
Async XLA Ops:
  7.2 520.5 %all-reduce.4.cloned.1.call-start = ((), (), s32[]{:S(2)}) async-start(), calls=%async_computation | async-start | bytes 3538944 | tf_op jit(solution)/shard_map/psum | solution.py:116
  7.2 6.6 %collective-permute-start = (bf16[2,8,32,128]{3,2,1,0:T(8,128)(2,1)}, bf16[2,8,32,128]{3,2,1,0:T(8,128)(2,1)S(1)}, u32[]{:S(2)}, u32[]{:S(2)}) collective-permute-start(bf16[2,8,32,128]{3,2,1,0:T(8,128)(2,1)} %bitcast.458), channel_id=1, source_target_pairs={{0,2},{2,4},{4,6},{6,8},{8,10},{10,12},{12,14},{14,16},{16,18},{18... | collective-permute-start | bytes 393224 | tf_op jit(solution)/shard_map/ppermute | solution.py:27
  14.6 8.4 %collective-permute-start.1 = (bf16[4,1,32,128]{3,2,1,0:T(8,128)(2,1)S(1)}, bf16[4,1,32,128]{3,2,1,0:T(8,128)(2,1)S(1)}, u32[]{:S(2)}, u32[]{:S(2)}) collective-permute-start(bf16[4,1,32,128]{3,2,1,0:T(8,128)(2,1)S(1)} %get-tuple-element.76), channel_id=1, source_target_pairs={{0,1},{2,3},{4,5},{6,7},{8,9},{10,11},{12,13},{14,15},{16,17},{18,... | collective-permute-start | bytes 98312 | tf_op jit(solution)/shard_map/ppermute | solution.py:15
  15.9 7.2 %collective-permute-start.2 = (bf16[4,1,32,128]{3,2,1,0:T(8,128)(2,1)S(1)}, bf16[4,1,32,128]{3,2,1,0:T(8,128)(2,1)S(1)}, u32[]{:S(2)}, u32[]{:S(2)}) collective-permute-start(bf16[4,1,32,128]{3,2,1,0:T(8,128)(2,1)S(1)} %get-tuple-element.77), channel_id=1, source_target_pairs={{1,0},{3,2},{5,4},{7,6},{9,8},{11,10},{13,12},{15,14},{17,16},{19,... | collective-permute-start | bytes 98312 | tf_op jit(solution)/shard_map/ppermute | solution.py:17
  24.1 1.2 copy-start
  24.5 1.7 copy-start.1
  29.4 0.9 copy-start.2
  29.4 0.9 copy-start.3
  35.1 7.6 %collective-permute-start.3 = (bf16[2,8,32,128]{3,2,1,0:T(8,128)(2,1)S(1)}, bf16[2,8,32,128]{3,2,1,0:T(8,128)(2,1)S(1)}, u32[]{:S(2)}, u32[]{:S(2)}) collective-permute-start(bf16[2,8,32,128]{3,2,1,0:T(8,128)(2,1)S(1)} %get-tuple-element.11), channel_id=1, source_target_pairs={{2,0},{4,2},{6,4},{8,6},{10,8},{12,10},{14,12},{16,14},{18,16},{20... | collective-permute-start | bytes 393224 | tf_op jit(solution)/shard_map/ppermute | solution.py:27
  42.8 117.9 %collective-permute-start.4 = (bf16[4,1,32,128]{3,2,1,0:T(8,128)(2,1)S(1)}, bf16[4,1,32,128]{3,2,1,0:T(8,128)(2,1)S(1)}, u32[]{:S(2)}, u32[]{:S(2)}) collective-permute-start(bf16[4,1,32,128]{3,2,1,0:T(8,128)(2,1)S(1)} %get-tuple-element.72), channel_id=1, source_target_pairs={{0,1},{2,3},{4,5},{6,7},{8,9},{10,11},{12,13},{14,15},{16,17},{18,... | collective-permute-start | bytes 98312 | tf_op jit(solution)/shard_map/ppermute | solution.py:15
  44.1 116.6 %collective-permute-start.5 = (bf16[4,1,32,128]{3,2,1,0:T(8,128)(2,1)S(1)}, bf16[4,1,32,128]{3,2,1,0:T(8,128)(2,1)S(1)}, u32[]{:S(2)}, u32[]{:S(2)}) collective-permute-start(bf16[4,1,32,128]{3,2,1,0:T(8,128)(2,1)S(1)} %get-tuple-element.73), channel_id=1, source_target_pairs={{1,0},{3,2},{5,4},{7,6},{9,8},{11,10},{13,12},{15,14},{17,16},{19,... | collective-permute-start | bytes 98312 | tf_op jit(solution)/shard_map/ppermute | solution.py:17
Sparse Core Ops, SparseCore 0:
  48.6 478.9 all-reduce.3
where the time goes:
time: 538 us; the launch traced here: 537 us
  waiting for transfers between devices  364 us (68%)
  blocking collectives  112 us (21%)
  starting transfers between devices  17.6 us (3%)
  matrix products  17 us (3%)
  between operations  14.9 us (3%)
  other arithmetic  7.14 us (1%)
    psum x1, waiting for transfers between devices, on_device(): lax.psum((kern_grad, bias_terms), ('dp', 'tm', 'space'))  360 us
    psum x1, blocking collectives, on_device(): lax.psum((kern_grad, bias_terms), ('dp', 'tm', 'space'))  112 us
  transfers between devices with their start and end apart: 7, of which 3 were waited for; matrix products, arithmetic and copies ran while one was open for 3% of the time, Pallas kernels for 0%

commit v1 on v0

v1 whole, which is shorter than its diff:
```python
import functools

import jax
import jax.numpy as jnp
from jax import lax
from jax.experimental import pallas as pl
from jax.experimental.pallas import tpu as pltpu
from jax.sharding import PartitionSpec as P

MESH = pl.DeviceIdType.MESH
Z_LO = 4
HALF = 64
ROWS = 28 * HALF
BIAS_ROW = 27 * HALF


def scalar_mask(ends, frame, lag):
    def clip(t):
        return sum((t >= end).astype(jnp.int32) for end in ends)

    earlier = frame - lag
    same = (clip(earlier) == clip(frame)) & (earlier >= 0)
    return same.astype(jnp.float32)


def scaled(values, mask):
    return values * jnp.full(values.shape, mask, jnp.float32).astype(values.dtype)


def column_sum(parts, back):
    count = parts.shape[0]
    col = lax.broadcasted_iota(jnp.int32, (count, 128), 0) % 32
    first, mid, last = parts[:, :128], parts[:, 128:256], parts[:, 256:]
    down, up = (last, first) if back else (first, last)
    down = jnp.where(col == 0, 0.0, pltpu.roll(down, 1, 0))
    up = jnp.where(col == 31, 0.0, pltpu.roll(up, count - 1, 0))
    return mid + down + up


def chip_kernel(
    dims, lens, x_hbm, w_hbm, bias_ref, cot_hbm,
    out_ref, ig_ref, full,
    xs, xt, lt, dzs, wv, cotv, yacc, part, rsbuf, zs, zbuf,
    loc, xsend, xrecv, dsend, drecv, rs_send, rs_recv, z_send, z_recv,
    zg_send, zg_recv, pg_send, pg_recv, cg_send, cg_recv,
):
    zh_n, tm_n = dims
    z_n, p_n = zh_n * Z_LO, tm_n // Z_LO
    chunk = ROWS // p_n
    tiles = chunk // 16
    group = max(1, tiles // z_n)
    owners = tiles // group
    stride = z_n // owners
    piece = group * 16

    dp, tm, core = lax.axis_index("dp"), lax.axis_index("tm"), lax.axis_index("space")
    other = 1 - core
    p, zl = tm // Z_LO, tm % Z_LO
    z = dp * Z_LO + zl
    after, before = (tm + 1) % tm_n, (tm + tm_n - 1) % tm_n

    def plane_dev(q):
        return (dp, q * Z_LO + zl, core)

    def z_dev(w):
        return (w // Z_LO, p * Z_LO + w % Z_LO, core)

    barrier = pltpu.get_barrier_semaphore()

    def greet(device):
        pl.semaphore_signal(barrier, inc=1, device_id=device, device_id_type=MESH)

    def remote(src, dst, send, recv, device):
        return pltpu.make_async_remote_copy(
            src_ref=src, dst_ref=dst, send_sem=send, recv_sem=recv, device_id=device, device_id_type=MESH
        )

    own = pl.ds(1 + 8 * core, 8)
    edge_row = 7 * other
    edge = pl.ds(1 + 8 * core + edge_row, 1)
    inner = pl.ds(1 + 9 * core, 7)

    for f in range(4):
        for r in (0, 17):
            xs[f, r] = jnp.zeros((32, 128), jnp.bfloat16)
            dzs[f, r] = jnp.zeros((32, 128), jnp.bfloat16)
    get_x = pltpu.make_async_copy(x_hbm.at[0], xs.at[pl.ds(2, 2), own], loc.at[0])
    get_w = pltpu.make_async_copy(w_hbm, wv, loc.at[1])
    get_cot = pltpu.make_async_copy(cot_hbm.at[0], cotv, loc.at[2])
    get_x.start()
    get_w.start()
    get_cot.start()

    greet((dp, tm, other))
    for near in (before, after):
        greet((dp, near, core))
        greet((dp, near, other))
    pl.loop(1, p_n)(lambda i: greet(plane_dev((p + i) % p_n)))
    pl.loop(1, z_n)(lambda i: greet(z_dev((z + i) % z_n)))
    pl.semaphore_wait(barrier, 5 + p_n - 1 + z_n - 1)

    x_next = remote(x_hbm.at[0], xs.at[pl.ds(0, 2), own], xsend.at[1], xrecv.at[1], (dp, after, core))
    x_edge = remote(
        x_hbm.at[0, pl.ds(0, 2), pl.ds(edge_row, 1)], xs.at[pl.ds(0, 2), edge],
        xsend.at[2], xrecv.at[2], (dp, after, other),
    )
    x_pair = remote(x_hbm.at[0], xs.at[pl.ds(2, 2), own], xsend.at[0], xrecv.at[0], (dp, tm, other))
    x_fwd = remote(
        xs.at[pl.ds(0, 2), inner], xs.at[pl.ds(0, 2), inner], xsend.at[3], xrecv.at[3], (dp, tm, other)
    )
    x_next.start()
    x_edge.start()
    x_pair.start()

    ends = [lens[0, 0]]
    for j in range(1, lens.shape[1]):
        ends.append(ends[-1] + lens[0, j])
    base = 2 * tm
    m0 = [scalar_mask(ends, base + t, 2) for t in range(4)]
    m1 = [scalar_mask(ends, base + t, 1) for t in range(3)]

    def x_rows(f):
        return jnp.concatenate(
            [xs[f, pl.ds(8 * core + a, 8)].reshape(256, 128) for a in range(3)], axis=1
        )

    def w_fwd(k):
        return jnp.concatenate(
            [jnp.concatenate([wv[k, a, b] for b in range(3)], axis=1) for a in range(3)], axis=0
        )

    def mm(lhs, rhs):
        return jnp.dot(lhs, rhs, preferred_element_type=jnp.float32)

    def turned(f):
        xt[...] = xs[f, pl.ds(1, 16)].reshape(512, 128).astype(jnp.float32).T
        mid = xt[pl.ds(pl.multiple_of(HALF * core, HALF), HALF), :]
        col = lax.broadcasted_iota(jnp.int32, (HALF, 512), 1) % 32
        left = jnp.where(col == 0, 0.0, pltpu.roll(mid, 1, 1))
        right = jnp.where(col == 31, 0.0, pltpu.roll(mid, 511, 1))
        block = jnp.concatenate([left, mid, right], axis=0)
        for t in range(2):
            k = f - t
            if k < 0 or k > 2:
                continue
            kept = block if k == 2 else block * (m1[t] if k == 1 else m0[t])
            lt[k, :, pl.ds(512 * t, 512)] = kept.astype(jnp.bfloat16)

    get_x.wait()
    get_w.wait()
    x_pair.wait_recv()
    yacc[0] = mm(x_rows(2), w_fwd(2))
    yacc[1] = mm(
        jnp.concatenate([x_rows(3), scaled(x_rows(2), m1[1])], axis=1),
        jnp.concatenate([w_fwd(2), w_fwd(1)], axis=0),
    )
    turned(2)
    turned(3)
    get_cot.wait()

    x_next.wait_recv()
    x_fwd.start()
    x_edge.wait_recv()
    yacc[0] += mm(
        jnp.concatenate([scaled(x_rows(1), m1[0]), scaled(x_rows(0), m0[0])], axis=1),
        jnp.concatenate([w_fwd(1), w_fwd(0)], axis=0),
    )
    yacc[1] += mm(scaled(x_rows(1), m0[1]), w_fwd(0))

    bias_part = jnp.zeros((16, 128), jnp.float32)
    for f in range(2):
        zed = column_sum(yacc[f], False) + bias_ref[...]
        sig = jax.nn.sigmoid(zed)
        out_ref[0, f] = (zed * sig).astype(jnp.bfloat16).reshape(8, 32, 128)
        cot = cotv[f].reshape(256, 128).astype(jnp.float32)
        dz = (cot * sig * (1.0 + zed * (1.0 - sig))).astype(jnp.bfloat16)
        dzs[f, own] = dz.reshape(8, 32, 128)
        bias_part += jnp.sum(dz.astype(jnp.float32).reshape(16, 16, 128), axis=0)

    two, later = pl.ds(0, 2), pl.ds(2, 2)
    d_pair = remote(dzs.at[two, own], dzs.at[two, own], dsend.at[0], drecv.at[0], (dp, tm, other))
    d_next = remote(dzs.at[two, own], dzs.at[later, own], dsend.at[1], drecv.at[1], (dp, before, core))
    d_edge = remote(dzs.at[two, edge], dzs.at[later, edge], dsend.at[2], drecv.at[2], (dp, before, other))
    d_pair.start()
    d_next.start()
    d_edge.start()

    part[pl.ds(BIAS_ROW, 16), :] = bias_part.astype(jnp.bfloat16)
    part[pl.ds(BIAS_ROW + 16, ROWS - BIAS_ROW - 16), :] = jnp.zeros((ROWS - BIAS_ROW - 16, 128), jnp.bfloat16)
    x_fwd.wait_recv()
    turned(0)
    turned(1)
    d_pair.wait_recv()

    right_side = jnp.concatenate(
        [
            jnp.concatenate([dzs[t, pl.ds(2 - a, 16)].reshape(512, 128) for a in range(3)], axis=1)
            for t in range(2)
        ],
        axis=0,
    )

    def chunk_rows(q):
        return pl.ds(pl.multiple_of(q * chunk, 16), chunk)

    def rs_copy(q):
        return remote(
            part.at[chunk_rows(q)], rsbuf.at[p], rs_send.at[q], rs_recv.at[p], plane_dev(q)
        )

    def rs_start(q):
        @pl.when(q != p)
        def _():
            rs_copy(q).start()

    sent = 0
    for k in range(3):
        grad = mm(lt[k], right_side)
        for a in range(3):
            for b in range(3):
                tap = (k * 3 + a) * 3 + b
                part[pl.ds(tap * HALF, HALF), :] = grad[
                    b * HALF : (b + 1) * HALF, a * 128 : (a + 1) * 128
                ].astype(jnp.bfloat16)
        ready = p_n if k == 2 else (k + 1) * 9 * HALF // chunk
        pl.loop(sent, ready)(rs_start)
        sent = ready
    rsbuf[pl.ds(p, 1)] = part[chunk_rows(p), :][None]

    def d_rows(f):
        return jnp.concatenate(
            [dzs[f, pl.ds(8 * core + 2 - a, 8)].reshape(256, 128) for a in range(3)], axis=1
        )

    def w_back(k):
        return jnp.concatenate([wv[k, a].reshape(384, 128) for a in range(3)], axis=1)

    def mm_t(lhs, rhs):
        return lax.dot_general(lhs, rhs, (((1,), (1,)), ((), ())), preferred_element_type=jnp.float32)

    yacc[0] = mm_t(
        jnp.concatenate([d_rows(0), scaled(d_rows(1), m1[1])], axis=1),
        jnp.concatenate([w_back(2), w_back(1)], axis=1),
    )
    yacc[1] = mm_t(d_rows(1), w_back(2))

    @pl.loop(1, p_n)
    def _(i):
        q = (p + i) % p_n
        remote(part.at[chunk_rows(q)], rsbuf.at[q], rs_send.at[q], rs_recv.at[q], plane_dev(q)).wait_recv()

    total = rsbuf[0].astype(jnp.float32)
    for q in range(1, p_n):
        total += rsbuf[q].astype(jnp.float32)
    zs[...] = total.astype(jnp.bfloat16)

    phase = core % stride

    def owner_of(j):
        return stride * j + phase

    def z_copy(j):
        return remote(
            zs.at[pl.ds(pl.multiple_of(j * piece, 16), piece)], zbuf.at[z], z_send.at[j], z_recv.at[z],
            z_dev(owner_of(j)),
        )

    @pl.loop(0, owners)
    def _(j):
        @pl.when(owner_of(j) != z)
        def _():
            z_copy(j).start()

    d_next.wait_recv()
    d_edge.wait_recv()
    yacc[0] += mm_t(scaled(d_rows(2), m0[2]), w_back(0))
    yacc[1] += mm_t(
        jnp.concatenate([scaled(d_rows(2), m1[2]), scaled(d_rows(3), m0[3])], axis=1),
        jnp.concatenate([w_back(1), w_back(0)], axis=1),
    )
    for f in range(2):
        ig_ref[0, f] = column_sum(yacc[f], True).astype(jnp.bfloat16).reshape(8, 32, 128)

    mine = (z - phase) // stride
    is_owner = ((z + stride - phase) % stride == 0) & (mine < owners)

    def piece_rows(j):
        return pl.ds(pl.multiple_of(p * chunk + j * piece, 16), piece)

    def zg_copy(j, w):
        return remote(
            full.at[core, piece_rows(j)], full.at[core, piece_rows(j)], zg_send.at[w], zg_recv.at[j], z_dev(w)
        )

    @pl.when(is_owner)
    def _():
        zbuf[pl.ds(z, 1)] = zs[pl.ds(pl.multiple_of(mine * piece, 16), piece), :][None]

        @pl.loop(1, z_n)
        def _(i):
            w = (z + i) % z_n
            remote(
                zs.at[pl.ds(0, piece)], zbuf.at[w], z_send.at[0], z_recv.at[w], z_dev(w)
            ).wait_recv()

        acc = zbuf[0].astype(jnp.float32)
        for w in range(1, z_n):
            acc += zbuf[w].astype(jnp.float32)
        full[core, piece_rows(mine)] = acc.astype(jnp.bfloat16)
        pl.loop(1, z_n)(lambda i: zg_copy(mine, (z + i) % z_n).start())

    @pl.loop(0, owners)
    def _(j):
        @pl.when(owner_of(j) != z)
        def _():
            zg_copy(j, owner_of(j)).wait_recv()

    def pg_copy(q, owner):
        return remote(
            full.at[core, chunk_rows(owner)], full.at[core, chunk_rows(owner)],
            pg_send.at[q], pg_recv.at[owner], plane_dev(q),
        )

    def cg_copy(q, side):
        return remote(
            full.at[side, chunk_rows(q)], full.at[side, chunk_rows(q)],
            cg_send.at[q], cg_recv.at[q], (dp, tm, other),
        )

    pl.loop(1, p_n)(lambda i: pg_copy((p + i) % p_n, p).start())
    cg_copy(p, core).start()

    @pl.loop(1, p_n)
    def _(i):
        q = (p + i) % p_n
        pg_copy(q, q).wait_recv()
        cg_copy(q, core).start()

    pl.loop(0, p_n)(lambda q: cg_copy(q, other).wait_recv())

    for copy in (x_next, x_edge, x_pair, x_fwd, d_pair, d_next, d_edge):
        copy.wait_send()

    @pl.loop(1, p_n)
    def _(i):
        q = (p + i) % p_n
        rs_copy(q).wait_send()
        pg_copy(q, p).wait_send()

    pl.loop(0, p_n)(lambda q: cg_copy(q, core).wait_send())

    @pl.loop(0, owners)
    def _(j):
        @pl.when(owner_of(j) != z)
        def _():
            z_copy(j).wait_send()

    @pl.when(is_owner)
    def _():
        pl.loop(1, z_n)(lambda i: zg_copy(mine, (z + i) % z_n).wait_send())


def on_device(dims, inputs, clip_lengths, weight, bias, cotangent):
    zh_n, tm_n = dims
    z_n, p_n = zh_n * Z_LO, tm_n // Z_LO
    chunk = ROWS // p_n
    tiles = chunk // 16
    piece = 16 * max(1, tiles // z_n)
    owners = chunk // piece
    block = inputs.shape
    dma = pltpu.SemaphoreType.DMA
    vmem, hbm, smem = (pl.BlockSpec(memory_space=m) for m in (pltpu.VMEM, pl.ANY, pltpu.SMEM))
    result, in_grad, full = pl.pallas_call(
        functools.partial(chip_kernel, dims),
        out_shape=(
            jax.ShapeDtypeStruct(block, jnp.bfloat16),
            jax.ShapeDtypeStruct(block, jnp.bfloat16),
            jax.ShapeDtypeStruct((2, ROWS, 128), jnp.bfloat16),
        ),
        in_specs=[smem, hbm, hbm, vmem, hbm],
        out_specs=(vmem, vmem, vmem),
        scratch_shapes=[
            pltpu.VMEM((4, 18, 32, 128), jnp.bfloat16),
            pltpu.VMEM((128, 512), jnp.float32),
            pltpu.VMEM((3, 3 * HALF, 1024), jnp.bfloat16),
            pltpu.VMEM((4, 18, 32, 128), jnp.bfloat16),
            pltpu.VMEM((3, 3, 3, 128, 128), jnp.bfloat16),
            pltpu.VMEM((2, 8, 32, 128), jnp.bfloat16),
            pltpu.VMEM((2, 256, 384), jnp.float32),
            pltpu.VMEM((ROWS, 128), jnp.bfloat16),
            pltpu.VMEM((p_n, chunk, 128), jnp.bfloat16),
            pltpu.VMEM((chunk, 128), jnp.bfloat16),
            pltpu.VMEM((z_n, piece, 128), jnp.bfloat16),
            dma((3,)), dma((4,)), dma((4,)), dma((3,)), dma((3,)),
            dma((p_n,)), dma((p_n,)), dma((owners,)), dma((z_n,)),
            dma((z_n,)), dma((owners,)), dma((p_n,)), dma((p_n,)), dma((p_n,)), dma((p_n,)),
        ],
        compiler_params=pltpu.CompilerParams(
            collective_id=0, has_side_effects=True, vmem_limit_bytes=40 * 1024 * 1024
        ),
        name="chip_kernel",
    )(clip_lengths, inputs, weight, bias.reshape(1, 128), cotangent)
    taps = full[:, :BIAS_ROW].reshape(2, 27, HALF, 128).transpose(1, 0, 2, 3)
    kern_grad = taps.astype(jnp.float32).reshape(3, 3, 3, 128, 128)
    bias_grad = jnp.sum(full[:, BIAS_ROW : BIAS_ROW + 16].astype(jnp.float32), axis=(0, 1))
    return result, in_grad, kern_grad, bias_grad


def solution(mesh):
    dims = (mesh.shape["dp"], mesh.shape["tm"])
    return jax.shard_map(
        functools.partial(on_device, dims),
        mesh=mesh,
        in_specs=(
            P("dp", "tm", "space", None, None),
            P("dp", None),
            P(),
            P(),
            P("dp", "tm", "space", None, None),
        ),
        out_specs=(
            P("dp", "tm", "space", None, None),
            P("dp", "tm", "space", None, None),
            P(),
            P(),
        ),
        check_vma=False,
    )
```

time: 538 us -> 70.5 us (0.13)
  waiting for transfers between devices: 364 us -> 0 us
  blocking collectives: 112 us -> 0 us
  Pallas kernels: 0 us -> 61.9 us
  starting transfers between devices: 17.6 us -> 0 us
  matrix products: 17 us -> 0 us
  between operations: 14.9 us -> 0.67 us
  other arithmetic: 7.14 us -> 0.73 us
    psum x1 -> x0, waiting for transfers between devices: 360 us -> none  [on_device(): lax.psum((kern_grad, bias_terms), ('dp', 'tm', 'space'))]
    psum x1 -> x0, blocking collectives: 112 us -> none  [on_device(): lax.psum((kern_grad, bias_terms), ('dp', 'tm', 'space'))]
    pallas_call x0 -> x1, Pallas kernels: none -> 61.9 us  [on_device(): pl.pallas_call(functools.partial(chip_kernel, dims), out_shape=(jax.Shape...]
    ppermute x6 -> x0, starting transfers between devices: 17.6 us -> none  [the longest x2 9.31 us: with_halo(): lax.ppermute(head, axis, [((i + 1) % count, i) for i in range(ends)])]
    dot_general x81 -> x0, matrix products: 17 us -> none  [the longest x27 6.69 us: on_device(): lax.dot_general(piece, masked, (((0,), (0,)), ((), ())), preferred_elemen...]
  transfers between devices with their start and end apart: 7 -> 0, of which waited for: 3 -> 0; matrix products, arithmetic and copies ran while one was open for 3% -> 0% of each run, Pallas kernels for 0% -> 0%
where the time goes in v1:
time: 70.5 us; the launch traced here: 70.3 us
  Pallas kernels  61.9 us (88%)
  local copies, waits for them, and re-layouts  7.06 us (10%)
  other arithmetic  0.73 us (1%)
    pallas_call x1, Pallas kernels, on_device(): pl.pallas_call(functools.partial(chip_kernel, dims), out_shape=(jax.Shape...  61.9 us
    unnamed x12, local copies, waits for them, and re-layouts  5.59 us
    reshape x1, local copies, waits for them, and re-layouts, on_device(): kern_grad = taps.astype(jnp.float32).reshape(3, 3, 3, 128, 128)  1.42 us

profile of v1, /device:TPU:1, one launch (start us, length us, event | category | flops | bytes accessed | tf_op | source)
XLA Modules:
  0.0 70.3 jit_solution(11999909578022564971)
XLA Ops:
  0.6 0.0 copy-start
  0.6 1.2 %copy-done = bf16[3,3,3,128,128]{4,3,2,1,0:T(8,128)(2,1)S(1)} copy-done((bf16[3,3,3,128,128]{4,3,2,1,0:T(8,128)(2,1)S(1)}, bf16[3,3,3,128,128]{4,3,2,1,0:T(8,128)(2,1)}, u32[]{:S(2)}) %copy-start) | copy-done | bytes 884760
  1.8 0.0 copy-start.1
  1.8 0.9 %copy-done.1 = bf16[1,2,8,32,128]{4,3,2,1,0:T(8,128)(2,1)S(1)} copy-done((bf16[1,2,8,32,128]{4,3,2,1,0:T(8,128)(2,1)S(1)}, bf16[1,2,8,32,128]{4,3,2,1,0:T(8,128)(2,1)}, u32[]{:S(2)}) %copy-start.1) | copy-done | bytes 131096
  2.7 0.0 copy-start.2
  2.7 0.9 %copy-done.2 = bf16[1,2,8,32,128]{4,3,2,1,0:T(8,128)(2,1)S(1)} copy-done((bf16[1,2,8,32,128]{4,3,2,1,0:T(8,128)(2,1)S(1)}, bf16[1,2,8,32,128]{4,3,2,1,0:T(8,128)(2,1)}, u32[]{:S(2)}) %copy-start.2) | copy-done | bytes 131096
  3.6 0.0 copy-start.3
  3.6 0.7 copy-done.3
  4.3 0.0 copy-start.4
  4.3 0.7 copy-done.4
  4.9 61.9 %chip_kernel.1 = (bf16[1,2,8,32,128]{4,3,2,1,0:T(8,128)(2,1)S(1)}, bf16[1,2,8,32,128]{4,3,2,1,0:T(8,128)(2,1)S(1)}, bf16[2,1792,128]{2,1,0:T(8,128)(2,1)S(1)}) custom-call(s32[1,4]{1,0:T(1,128)S(1)} %copy-done.3, bf16[1,2,8,32,128]{4,3,2,1,0:T(8,128)(2,1)S(1)} %copy-done.1, bf16[3,3,3,128,128]{4,3,2,1,0:T(8,128)(2,1)S(1)} %copy-done, f32[1,128]{1,0:T(1,128)S(1)} %bitcast.6, ...), custom_call_target="tpu_custom_call" | custom-call | tf_op jit(solution)/shard_map/chip_kernel/pallas_call | solution.py:373
  66.8 0.5 convert_reduce_fusion
  67.3 0.1 slice.6
  67.4 0.2 convert_bitcast_fusion
  67.6 1.4 %copy.9 = f32[27,2,64,128]{3,2,1,0:T(8,128)} copy(f32[27,2,64,128]{3,2,0,1:T(8,128)S(1)} %convert_bitcast_fusion) | data formatting | bytes 3538944 | tf_op jit(solution)/shard_map/reshape | solution.py:404
  69.0 0.7 copy.12
  69.7 0.7 copy.13
Async XLA Ops:
  0.6 1.2 %copy-start = (bf16[3,3,3,128,128]{4,3,2,1,0:T(8,128)(2,1)S(1)}, bf16[3,3,3,128,128]{4,3,2,1,0:T(8,128)(2,1)}, u32[]{:S(2)}) copy-start(bf16[3,3,3,128,128]{4,3,2,1,0:T(8,128)(2,1)} %w_hbm.1) | copy-start | bytes 2654212
  1.8 0.9 %copy-start.1 = (bf16[1,2,8,32,128]{4,3,2,1,0:T(8,128)(2,1)S(1)}, bf16[1,2,8,32,128]{4,3,2,1,0:T(8,128)(2,1)}, u32[]{:S(2)}) copy-start(bf16[1,2,8,32,128]{4,3,2,1,0:T(8,128)(2,1)} %x_hbm.1) | copy-start | bytes 393220
  2.7 0.9 %copy-start.2 = (bf16[1,2,8,32,128]{4,3,2,1,0:T(8,128)(2,1)S(1)}, bf16[1,2,8,32,128]{4,3,2,1,0:T(8,128)(2,1)}, u32[]{:S(2)}) copy-start(bf16[1,2,8,32,128]{4,3,2,1,0:T(8,128)(2,1)} %cot_hbm.1) | copy-start | bytes 393220
  3.6 0.7 copy-start.3
  4.3 0.7 copy-start.4

commit v2 on v1

v2 whole, which is shorter than its diff:
```python
import functools

import jax
import jax.numpy as jnp
from jax import lax
from jax.experimental import pallas as pl
from jax.experimental.pallas import tpu as pltpu
from jax.sharding import PartitionSpec as P

MESH = pl.DeviceIdType.MESH
Z_LO = 4
HALF = 64
ROWS = 28 * HALF
BIAS_ROW = 27 * HALF


def scalar_mask(ends, frame, lag):
    def clip(t):
        return sum((t >= end).astype(jnp.int32) for end in ends)

    earlier = frame - lag
    same = (clip(earlier) == clip(frame)) & (earlier >= 0)
    return same.astype(jnp.float32)


def scaled(values, mask):
    return values * jnp.full(values.shape, mask, jnp.float32).astype(values.dtype)


def column_sum(parts, back):
    count = parts.shape[0]
    col = lax.broadcasted_iota(jnp.int32, (count, 128), 0) % 32
    first, mid, last = parts[:, :128], parts[:, 128:256], parts[:, 256:]
    down, up = (last, first) if back else (first, last)
    down = jnp.where(col == 0, 0.0, pltpu.roll(down, 1, 0))
    up = jnp.where(col == 31, 0.0, pltpu.roll(up, count - 1, 0))
    return mid + down + up


def chip_kernel(
    dims, lens_hbm, x_hbm, w_hbm, bias_hbm, cot_hbm,
    out_ref, ig_ref, full,
    lens, bias, xs, xt, lt, dzs, wv, cotv, yacc, part, rsbuf, zs, zbuf,
    loc, xsend, xrecv, dsend, drecv, rs_send, rs_recv, z_send, z_recv,
    zg_send, zg_recv, pg_send, pg_recv, cg_send, cg_recv,
):
    zh_n, tm_n = dims
    z_n, p_n = zh_n * Z_LO, tm_n // Z_LO
    chunk, piece, owners = pieces(dims)

    dp, tm, core = lax.axis_index("dp"), lax.axis_index("tm"), lax.axis_index("space")
    other = 1 - core
    p, zl = tm // Z_LO, tm % Z_LO
    z = dp * Z_LO + zl
    after, before = (tm + 1) % tm_n, (tm + tm_n - 1) % tm_n

    def plane_dev(q):
        return (dp, q * Z_LO + zl, core)

    def z_dev(w):
        return (w // Z_LO, p * Z_LO + w % Z_LO, core)

    barrier = pltpu.get_barrier_semaphore()

    def greet(device):
        pl.semaphore_signal(barrier, inc=1, device_id=device, device_id_type=MESH)

    def remote(src, dst, send, recv, device):
        return pltpu.make_async_remote_copy(
            src_ref=src, dst_ref=dst, send_sem=send, recv_sem=recv, device_id=device, device_id_type=MESH
        )

    own = pl.ds(1 + 8 * core, 8)
    edge_row = 7 * other
    edge = pl.ds(1 + 8 * core + edge_row, 1)
    inner = pl.ds(1 + 9 * core, 7)
    two, later = pl.ds(0, 2), pl.ds(2, 2)

    greet((dp, tm, other))
    for near in (before, after):
        greet((dp, near, core))
        greet((dp, near, other))
    pl.loop(1, p_n)(lambda i: greet(plane_dev((p + i) % p_n)))
    pl.loop(1, z_n)(lambda i: greet(z_dev((z + i) % z_n)))

    get_x = pltpu.make_async_copy(x_hbm.at[0], xs.at[later, own], loc.at[0])
    get_w = pltpu.make_async_copy(w_hbm, wv, loc.at[1])
    get_cot = pltpu.make_async_copy(cot_hbm.at[0], cotv, loc.at[2])
    get_lens = pltpu.make_async_copy(lens_hbm, lens, loc.at[3])
    get_bias = pltpu.make_async_copy(bias_hbm, bias, loc.at[4])
    for copy in (get_x, get_w, get_lens, get_cot, get_bias):
        copy.start()
    for f in range(4):
        for r in (0, 17):
            xs[f, r] = jnp.zeros((32, 128), jnp.bfloat16)
            dzs[f, r] = jnp.zeros((32, 128), jnp.bfloat16)

    @pl.when(tm == 0)
    def _():
        xs[two, pl.ds(1, 16)] = jnp.zeros((2, 16, 32, 128), jnp.bfloat16)

    @pl.when(tm == tm_n - 1)
    def _():
        dzs[later, pl.ds(1, 16)] = jnp.zeros((2, 16, 32, 128), jnp.bfloat16)

    get_lens.wait()
    ends = [lens[0, 0]]
    for j in range(1, lens.shape[1]):
        ends.append(ends[-1] + lens[0, j])
    base = 2 * tm
    m0 = [scalar_mask(ends, base + t, 2) for t in range(4)]
    m1 = [scalar_mask(ends, base + t, 1) for t in range(3)]

    pl.semaphore_wait(barrier, 5 + p_n - 1 + z_n - 1)

    x_next = remote(x_hbm.at[0], xs.at[two, own], xsend.at[1], xrecv.at[1], (dp, after, core))
    x_edge = remote(
        x_hbm.at[0, two, pl.ds(edge_row, 1)], xs.at[two, edge], xsend.at[2], xrecv.at[2], (dp, after, other)
    )
    x_pair = remote(x_hbm.at[0], xs.at[later, own], xsend.at[0], xrecv.at[0], (dp, tm, other))
    x_fwd = remote(xs.at[two, inner], xs.at[two, inner], xsend.at[3], xrecv.at[3], (dp, tm, other))

    @pl.when(tm < tm_n - 1)
    def _():
        x_next.start()
        x_edge.start()

    x_pair.start()

    def x_rows(f):
        return jnp.concatenate(
            [xs[f, pl.ds(8 * core + a, 8)].reshape(256, 128) for a in range(3)], axis=1
        )

    def w_fwd(k):
        return jnp.concatenate(
            [jnp.concatenate([wv[k, a, b] for b in range(3)], axis=1) for a in range(3)], axis=0
        )

    def mm(lhs, rhs):
        return jnp.dot(lhs, rhs, preferred_element_type=jnp.float32)

    def turned(f):
        xt[...] = xs[f, pl.ds(1, 16)].reshape(512, 128).astype(jnp.float32).T
        mid = xt[pl.ds(pl.multiple_of(HALF * core, HALF), HALF), :]
        col = lax.broadcasted_iota(jnp.int32, (HALF, 512), 1) % 32
        left = jnp.where(col == 0, 0.0, pltpu.roll(mid, 1, 1))
        right = jnp.where(col == 31, 0.0, pltpu.roll(mid, 511, 1))
        block = jnp.concatenate([left, mid, right], axis=0)
        for t in range(2):
            k = f - t
            if k < 0 or k > 2:
                continue
            kept = block if k == 2 else block * (m1[t] if k == 1 else m0[t])
            lt[k, :, pl.ds(512 * t, 512)] = kept.astype(jnp.bfloat16)

    get_x.wait()
    get_w.wait()
    x_pair.wait_recv()
    yacc[0] = mm(x_rows(2), w_fwd(2))
    yacc[1] = mm(
        jnp.concatenate([x_rows(3), scaled(x_rows(2), m1[1])], axis=1),
        jnp.concatenate([w_fwd(2), w_fwd(1)], axis=0),
    )
    turned(2)
    turned(3)
    get_cot.wait()
    get_bias.wait()

    @pl.when(tm > 0)
    def _():
        x_next.wait_recv()
        x_fwd.start()
        x_edge.wait_recv()

    yacc[0] += mm(
        jnp.concatenate([scaled(x_rows(1), m1[0]), scaled(x_rows(0), m0[0])], axis=1),
        jnp.concatenate([w_fwd(1), w_fwd(0)], axis=0),
    )
    yacc[1] += mm(scaled(x_rows(1), m0[1]), w_fwd(0))

    bias_part = jnp.zeros((16, 128), jnp.float32)
    for f in range(2):
        zed = column_sum(yacc[f], False) + bias[...]
        sig = jax.nn.sigmoid(zed)
        out_ref[0, f] = (zed * sig).astype(jnp.bfloat16).reshape(8, 32, 128)
        cot = cotv[f].reshape(256, 128).astype(jnp.float32)
        dz = (cot * sig * (1.0 + zed * (1.0 - sig))).astype(jnp.bfloat16)
        dzs[f, own] = dz.reshape(8, 32, 128)
        bias_part += jnp.sum(dz.astype(jnp.float32).reshape(16, 16, 128), axis=0)

    d_pair = remote(dzs.at[two, own], dzs.at[two, own], dsend.at[0], drecv.at[0], (dp, tm, other))
    d_next = remote(dzs.at[two, own], dzs.at[later, own], dsend.at[1], drecv.at[1], (dp, before, core))
    d_edge = remote(dzs.at[two, edge], dzs.at[later, edge], dsend.at[2], drecv.at[2], (dp, before, other))
    d_pair.start()

    @pl.when(zl > 0)
    def _():
        d_next.start()
        d_edge.start()

    part[pl.ds(BIAS_ROW, 16), :] = bias_part.astype(jnp.bfloat16)
    part[pl.ds(BIAS_ROW + 16, ROWS - BIAS_ROW - 16), :] = jnp.zeros((ROWS - BIAS_ROW - 16, 128), jnp.bfloat16)
    pl.when(tm > 0)(x_fwd.wait_recv)
    turned(0)
    turned(1)
    d_pair.wait_recv()

    right_side = jnp.concatenate(
        [
            jnp.concatenate([dzs[t, pl.ds(2 - a, 16)].reshape(512, 128) for a in range(3)], axis=1)
            for t in range(2)
        ],
        axis=0,
    )

    def chunk_rows(q):
        return pl.ds(pl.multiple_of(q * chunk, 16), chunk)

    def rs_start(q):
        @pl.when(q != p)
        def _():
            slot = (p + p_n - q - 1) % p_n
            remote(part.at[chunk_rows(q)], rsbuf.at[slot], rs_send, rs_recv, plane_dev(q)).start()

    sent = 0
    for k in range(3):
        grad = mm(lt[k], right_side)
        for a in range(3):
            for b in range(3):
                tap = (k * 3 + a) * 3 + b
                part[pl.ds(tap * HALF, HALF), :] = grad[
                    b * HALF : (b + 1) * HALF, a * 128 : (a + 1) * 128
                ].astype(jnp.bfloat16)
        ready = p_n if k == 2 else (k + 1) * 9 * HALF // chunk
        pl.loop(sent, ready)(rs_start)
        sent = ready

    def d_rows(f):
        return jnp.concatenate(
            [dzs[f, pl.ds(8 * core + 2 - a, 8)].reshape(256, 128) for a in range(3)], axis=1
        )

    def w_back(k):
        return jnp.concatenate([wv[k, a].reshape(384, 128) for a in range(3)], axis=1)

    def mm_t(lhs, rhs):
        return lax.dot_general(lhs, rhs, (((1,), (1,)), ((), ())), preferred_element_type=jnp.float32)

    yacc[0] = mm_t(
        jnp.concatenate([d_rows(0), scaled(d_rows(1), m1[1])], axis=1),
        jnp.concatenate([w_back(2), w_back(1)], axis=1),
    )
    yacc[1] = mm_t(d_rows(1), w_back(2))

    remote(rsbuf, rsbuf, rs_send, rs_recv, plane_dev(p)).wait_recv()
    total = part[chunk_rows(p), :].astype(jnp.float32)
    for q in range(p_n - 1):
        total += rsbuf[q].astype(jnp.float32)
    zs[...] = total.astype(jnp.bfloat16)

    def owner_of(j):
        return (z_n + j - owners // 2) % z_n

    mine = (z + owners // 2) % z_n
    is_owner = mine < owners

    def zs_rows(j):
        return pl.ds(pl.multiple_of(j * piece, 16), piece)

    @pl.loop(0, owners)
    def _(j):
        w = owner_of(j)

        @pl.when(w != z)
        def _():
            slot = (z + z_n - w - 1) % z_n
            remote(zs.at[zs_rows(j)], zbuf.at[slot], z_send, z_recv, z_dev(w)).start()

    @pl.when(zl == 0)
    def _():
        @pl.when(tm > 0)
        def _():
            d_next.start()
            d_edge.start()

    def piece_rows(owner, j):
        return pl.ds(pl.multiple_of(owner * chunk + j * piece, 16), piece)

    def zg_copy(j, w):
        return remote(
            full.at[core, piece_rows(p, j)], full.at[core, piece_rows(p, j)], zg_send, zg_recv.at[j], z_dev(w)
        )

    def pg_start(j):
        rows = piece_rows(p, j)

        @pl.loop(1, p_n)
        def _(i):
            remote(
                full.at[core, rows], full.at[core, rows], pg_send, pg_recv.at[p], plane_dev((p + i) % p_n)
            ).start()

    @pl.when(is_owner)
    def _():
        remote(zbuf, zbuf, z_send, z_recv, z_dev(z)).wait_recv()
        acc = zs[zs_rows(mine), :].astype(jnp.float32)
        for w in range(z_n - 1):
            acc += zbuf[w].astype(jnp.float32)
        full[core, piece_rows(p, mine)] = acc.astype(jnp.bfloat16)

        @pl.loop(0, z_n)
        def _(w):
            pl.when(w != z)(lambda: zg_copy(mine, w).start())

        pg_start(mine)

    for j in sorted(range(owners), key=lambda j: abs(j - owners // 2)):
        @pl.when(owner_of(j) != z)
        def _():
            zg_copy(j, owner_of(j)).wait_recv()
            pg_start(j)

    def cg_copy(rows):
        return remote(full.at[core, rows], full.at[core, rows], cg_send, cg_recv, (dp, tm, other))

    cg_copy(chunk_rows(p)).start()

    @pl.when(tm < tm_n - 1)
    def _():
        d_next.wait_recv()
        d_edge.wait_recv()

    yacc[0] += mm_t(scaled(d_rows(2), m0[2]), w_back(0))
    yacc[1] += mm_t(
        jnp.concatenate([scaled(d_rows(2), m1[2]), scaled(d_rows(3), m0[3])], axis=1),
        jnp.concatenate([w_back(1), w_back(0)], axis=1),
    )
    for f in range(2):
        ig_ref[0, f] = column_sum(yacc[f], True).astype(jnp.bfloat16).reshape(8, 32, 128)

    @pl.loop(1, p_n)
    def _(i):
        q = (p + i) % p_n
        rows = chunk_rows(q)
        remote(full.at[core, rows], full.at[core, rows], pg_send, pg_recv.at[q], plane_dev(q)).wait_recv()
        cg_copy(rows).start()

    @pl.when(tm < tm_n - 1)
    def _():
        x_next.wait_send()
        x_edge.wait_send()

    x_pair.wait_send()
    d_pair.wait_send()

    @pl.when(tm > 0)
    def _():
        x_fwd.wait_send()
        d_next.wait_send()
        d_edge.wait_send()

    rest = pl.ds(0, (p_n - 1) * chunk)
    remote(part.at[rest], part.at[rest], rs_send, rs_recv, plane_dev(p)).wait_send()

    @pl.when(is_owner)
    def _():
        most = zs.at[pl.ds(0, (owners - 1) * piece)]
        remote(most, most, z_send, z_recv, z_dev(z)).wait_send()
        remote(zbuf, zbuf, zg_send, z_recv, z_dev(z)).wait_send()

    @pl.when(jnp.logical_not(is_owner))
    def _():
        remote(zs, zs, z_send, z_recv, z_dev(z)).wait_send()

    remote(full.at[core, rest], full.at[core, rest], pg_send, pg_recv.at[p], plane_dev(p)).wait_send()
    everything = remote(full.at[core], full.at[other], cg_send, cg_recv, (dp, tm, other))
    everything.wait_send()
    everything.wait_recv()


def finish_kernel(out_in, ig_in, full, out_ref, ig_ref, grad_ref, bias_ref, buf, bias_buf, sems):
    copies = [
        pltpu.make_async_copy(out_in, out_ref, sems.at[0]),
        pltpu.make_async_copy(ig_in, ig_ref, sems.at[1]),
    ]
    for k in range(3):
        for a in range(3):
            for b in range(3):
                tap = (k * 3 + a) * 3 + b
                for side in range(2):
                    buf[k, a, b, pl.ds(side * HALF, HALF), :] = full[side, pl.ds(tap * HALF, HALF), :].astype(
                        jnp.float32
                    )
            copies.append(pltpu.make_async_copy(buf.at[k, a], grad_ref.at[k, a], sems.at[3 + 3 * k + a]))
            copies[-1].start()
    copies[0].start()
    copies[1].start()
    terms = full[:, pl.ds(BIAS_ROW, 16), :].astype(jnp.float32)
    bias_buf[...] = jnp.sum(terms[0] + terms[1], axis=0, keepdims=True)
    copies.append(pltpu.make_async_copy(bias_buf, bias_ref, sems.at[2]))
    copies[-1].start()
    for copy in copies:
        copy.wait()


def pieces(dims):
    zh_n, tm_n = dims
    z_n, p_n = zh_n * Z_LO, tm_n // Z_LO
    chunk = ROWS // p_n
    piece = 16 * max(1, chunk // 16 // z_n)
    return chunk, piece, chunk // piece


def on_device(dims, inputs, clip_lengths, weight, bias, cotangent):
    zh_n, tm_n = dims
    z_n, p_n = zh_n * Z_LO, tm_n // Z_LO
    chunk, piece, owners = pieces(dims)
    block = inputs.shape
    dma = pltpu.SemaphoreType.DMA
    vmem, hbm = (pl.BlockSpec(memory_space=m) for m in (pltpu.VMEM, pltpu.HBM))
    operands = (clip_lengths, inputs, weight, bias.reshape(1, 128), cotangent)
    result, in_grad, full = pl.pallas_call(
        functools.partial(chip_kernel, dims),
        out_shape=(
            jax.ShapeDtypeStruct(block, jnp.bfloat16),
            jax.ShapeDtypeStruct(block, jnp.bfloat16),
            jax.ShapeDtypeStruct((2, ROWS, 128), jnp.bfloat16),
        ),
        in_specs=[hbm, hbm, hbm, hbm, hbm],
        out_specs=(vmem, vmem, vmem),
        scratch_shapes=[
            pltpu.SMEM(clip_lengths.shape, jnp.int32),
            pltpu.VMEM((1, 128), jnp.float32),
            pltpu.VMEM((4, 18, 32, 128), jnp.bfloat16),
            pltpu.VMEM((128, 512), jnp.float32),
            pltpu.VMEM((3, 3 * HALF, 1024), jnp.bfloat16),
            pltpu.VMEM((4, 18, 32, 128), jnp.bfloat16),
            pltpu.VMEM((3, 3, 3, 128, 128), jnp.bfloat16),
            pltpu.VMEM((2, 8, 32, 128), jnp.bfloat16),
            pltpu.VMEM((2, 256, 384), jnp.float32),
            pltpu.VMEM((ROWS, 128), jnp.bfloat16),
            pltpu.VMEM((p_n - 1, chunk, 128), jnp.bfloat16),
            pltpu.VMEM((chunk, 128), jnp.bfloat16),
            pltpu.VMEM((z_n - 1, piece, 128), jnp.bfloat16),
            dma((5,)), dma((4,)), dma((4,)), dma((3,)), dma((3,)),
            dma, dma, dma, dma, dma, dma((owners,)), dma, dma((p_n,)), dma, dma,
        ],
        compiler_params=pltpu.CompilerParams(
            collective_id=0, has_side_effects=True, vmem_limit_bytes=40 * 1024 * 1024
        ),
        name="chip_kernel",
    )(*(pltpu.with_memory_space_constraint(a, pltpu.HBM) for a in operands))
    result, in_grad, kern_grad, bias_grad = pl.pallas_call(
        finish_kernel,
        out_shape=(
            jax.ShapeDtypeStruct(block, jnp.bfloat16),
            jax.ShapeDtypeStruct(block, jnp.bfloat16),
            jax.ShapeDtypeStruct((3, 3, 3, 128, 128), jnp.float32),
            jax.ShapeDtypeStruct((1, 128), jnp.float32),
        ),
        in_specs=[vmem, vmem, vmem],
        out_specs=(hbm, hbm, hbm, hbm),
        scratch_shapes=[
            pltpu.VMEM((3, 3, 3, 128, 128), jnp.float32),
            pltpu.VMEM((1, 128), jnp.float32),
            dma((12,)),
        ],
        compiler_params=pltpu.CompilerParams(vmem_limit_bytes=32 * 1024 * 1024),
        name="finish_kernel",
    )(result, in_grad, full)
    return result, in_grad, kern_grad, bias_grad.reshape(128)


def solution(mesh):
    dims = (mesh.shape["dp"], mesh.shape["tm"])
    return jax.shard_map(
        functools.partial(on_device, dims),
        mesh=mesh,
        in_specs=(
            P("dp", "tm", "space", None, None),
            P("dp", None),
            P(),
            P(),
            P("dp", "tm", "space", None, None),
        ),
        out_specs=(
            P("dp", "tm", "space", None, None),
            P("dp", "tm", "space", None, None),
            P(),
            P(),
        ),
        check_vma=False,
    )
```

time: 70.5 us -> 56.1 us (0.80)
  local copies, waits for them, and re-layouts: 7.06 us -> 0 us
  Pallas kernels: 61.9 us -> 55.4 us
  other arithmetic: 0.73 us -> 0 us
    pallas_call x1, Pallas kernels: 61.9 us -> 54 us  [on_device(): pl.pallas_call(functools.partial(chip_kernel, dims), out_shape=(jax.Shape...]
    unnamed x12 -> x0, local copies, waits for them, and re-layouts: 5.59 us -> none
    pallas_call x0 -> x1, Pallas kernels: none -> 1.42 us  [on_device(): pl.pallas_call(finish_kernel, out_shape=(jax.ShapeDtypeStruct(block, jnp....]
    reshape x1 -> x0, local copies, waits for them, and re-layouts: 1.42 us -> none  [on_device(): kern_grad = taps.astype(jnp.float32).reshape(3, 3, 3, 128, 128)]
where the time goes in v2:
time: 56.1 us; the launch traced here: 56 us
  Pallas kernels  55.4 us (99%)
  between operations  0.64 us (1%)
    pallas_call x1, Pallas kernels, on_device(): pl.pallas_call(functools.partial(chip_kernel, dims), out_shape=(jax.Shape...  54 us
    pallas_call x1, Pallas kernels, on_device(): pl.pallas_call(finish_kernel, out_shape=(jax.ShapeDtypeStruct(block, jnp....  1.42 us

profile of v2, /device:TPU:1, one launch (start us, length us, event | category | flops | bytes accessed | tf_op | source)
XLA Modules:
  0.0 56.0 jit_solution(4102784389092243271)
XLA Ops:
  0.6 54.0 %chip_kernel.1 = (bf16[1,2,8,32,128]{4,3,2,1,0:T(8,128)(2,1)S(1)}, bf16[1,2,8,32,128]{4,3,2,1,0:T(8,128)(2,1)S(1)}, bf16[2,1792,128]{2,1,0:T(8,128)(2,1)S(1)}) custom-call(s32[1,4]{1,0:T(1,128)} %lens_hbm.1, bf16[1,2,8,32,128]{4,3,2,1,0:T(8,128)(2,1)} %x_hbm.1, bf16[3,3,3,128,128]{4,3,2,1,0:T(8,128)(2,1)} %w_hbm.1, f32[1,128]{1,0:T(1,128)} %bitcast.2, ...), custom_call_target="tpu_custom_call" | custom-call | tf_op jit(solution)/shard_map/chip_kernel/pallas_call | solution.py:423
  54.6 1.4 %finish_kernel.1 = (bf16[1,2,8,32,128]{4,3,2,1,0:T(8,128)(2,1)}, bf16[1,2,8,32,128]{4,3,2,1,0:T(8,128)(2,1)}, f32[3,3,3,128,128]{4,3,2,1,0:T(8,128)}, f32[1,128]{1,0:T(1,128)}) custom-call(bf16[1,2,8,32,128]{4,3,2,1,0:T(8,128)(2,1)S(1)} %get-tuple-element.11.out_in, bf16[1,2,8,32,128]{4,3,2,1,0:T(8,128)(2,1)S(1)} %get-tuple-element.12.ig_in, ...), custom_call_target="tpu_custom_call" | custom-call | tf_op jit(solution)/shard_map/finish_kernel/pallas_call | solution.py:454

commit v3 on v2

--- a/solution.py
+++ b/solution.py
@@ -9,9 +9,18 @@
 
 MESH = pl.DeviceIdType.MESH
 Z_LO = 4
+PLANE_Y = 4
 HALF = 64
 ROWS = 28 * HALF
-BIAS_ROW = 27 * HALF
+TILES = 9 * HALF // 16
+
+
+def tile_row(p_n, k, tile):
+    chunk, per = ROWS // p_n, TILES // p_n
+    if k < 3 and tile < per * p_n:
+        return tile // per * chunk + (k * per + tile % per) * 16
+    extra = k * (TILES - per * p_n) + (tile - per * p_n if k < 3 else tile)
+    return extra % p_n * chunk + (3 * per + extra // p_n) * 16
 
 
 def scalar_mask(ends, frame, lag):
@@ -41,12 +50,13 @@
     dims, lens_hbm, x_hbm, w_hbm, bias_hbm, cot_hbm,
     out_ref, ig_ref, full,
     lens, bias, xs, xt, lt, dzs, wv, cotv, yacc, part, rsbuf, zs, zbuf,
-    loc, xsend, xrecv, dsend, drecv, rs_send, rs_recv, z_send, z_recv,
+    known, loc, xsend, xrecv, dsend, drecv, rs_send, rs_recv, z_send, z_recv,
     zg_send, zg_recv, pg_send, pg_recv, cg_send, cg_recv,
 ):
     zh_n, tm_n = dims
     z_n, p_n = zh_n * Z_LO, tm_n // Z_LO
     chunk, piece, owners = pieces(dims)
+    rounds = rounds_of(z_n)
 
     dp, tm, core = lax.axis_index("dp"), lax.axis_index("tm"), lax.axis_index("space")
     other = 1 - core
@@ -77,11 +87,15 @@
     two, later = pl.ds(0, 2), pl.ds(2, 2)
 
     greet((dp, tm, other))
-    for near in (before, after):
-        greet((dp, near, core))
-        greet((dp, near, other))
+    for there, near in ((tm > 0, before), (tm < tm_n - 1, after)):
+        @pl.when(there)
+        def _():
+            greet((dp, near, core))
+            greet((dp, near, other))
+
     pl.loop(1, p_n)(lambda i: greet(plane_dev((p + i) % p_n)))
-    pl.loop(1, z_n)(lambda i: greet(z_dev((z + i) % z_n)))
+    greet(z_dev((z + 1) % z_n))
+    greet(z_dev((z + z_n - 1) % z_n))
 
     get_x = pltpu.make_async_copy(x_hbm.at[0], xs.at[later, own], loc.at[0])
     get_w = pltpu.make_async_copy(w_hbm, wv, loc.at[1])
@@ -111,19 +125,37 @@
     m0 = [scalar_mask(ends, base + t, 2) for t in range(4)]
     m1 = [scalar_mask(ends, base + t, 1) for t in range(3)]
 
-    pl.semaphore_wait(barrier, 5 + p_n - 1 + z_n - 1)
-
-    x_next = remote(x_hbm.at[0], xs.at[two, own], xsend.at[1], xrecv.at[1], (dp, after, core))
+    get_x.wait()
+    sides = (tm + tm_n - 1) // tm_n + (2 * (tm_n - 1) - tm) // tm_n
+    pl.semaphore_wait(barrier, 1 + (p_n - 1) + 2 + 2 * sides)
+
+    def tell(r):
+        for w in (z + rounds[r], z + z_n - rounds[r]):
+            pl.semaphore_signal(known.at[r], inc=1, device_id=z_dev(w % z_n), device_id_type=MESH)
+
+    def hear(r):
+        pl.semaphore_wait(known.at[r], 2)
+
+    tell(0)
+
+    x_next = [
+        remote(xs.at[2 + f, own], xs.at[f, own], xsend.at[1 + 4 * f], xrecv.at[1 + 4 * f], (dp, after, core))
+        for f in range(2)
+    ]
     x_edge = remote(
-        x_hbm.at[0, two, pl.ds(edge_row, 1)], xs.at[two, edge], xsend.at[2], xrecv.at[2], (dp, after, other)
+        xs.at[later, edge], xs.at[two, edge], xsend.at[2], xrecv.at[2], (dp, after, other)
     )
-    x_pair = remote(x_hbm.at[0], xs.at[later, own], xsend.at[0], xrecv.at[0], (dp, tm, other))
-    x_fwd = remote(xs.at[two, inner], xs.at[two, inner], xsend.at[3], xrecv.at[3], (dp, tm, other))
+    x_pair = remote(xs.at[later, own], xs.at[later, own], xsend.at[0], xrecv.at[0], (dp, tm, other))
+    x_fwd = [
+        remote(xs.at[f, inner], xs.at[f, inner], xsend.at[3 + f], xrecv.at[3 + f], (dp, tm, other))
+        for f in range(2)
+    ]
 
     @pl.when(tm < tm_n - 1)
     def _():
-        x_next.start()
         x_edge.start()
+        x_next[1].start()
+        x_next[0].start()
 
     x_pair.start()
 
@@ -154,7 +186,6 @@
             kept = block if k == 2 else block * (m1[t] if k == 1 else m0[t])
             lt[k, :, pl.ds(512 * t, 512)] = kept.astype(jnp.bfloat16)
 
-    get_x.wait()
     get_w.wait()
     x_pair.wait_recv()
     yacc[0] = mm(x_rows(2), w_fwd(2))
@@ -167,44 +198,56 @@
     get_cot.wait()
     get_bias.wait()
 
-    @pl.when(tm > 0)
-    def _():
-        x_next.wait_recv()
-        x_fwd.start()
-        x_edge.wait_recv()
-
-    yacc[0] += mm(
-        jnp.concatenate([scaled(x_rows(1), m1[0]), scaled(x_rows(0), m0[0])], axis=1),
-        jnp.concatenate([w_fwd(1), w_fwd(0)], axis=0),
-    )
-    yacc[1] += mm(scaled(x_rows(1), m0[1]), w_fwd(0))
-
-    bias_part = jnp.zeros((16, 128), jnp.float32)
-    for f in range(2):
+    def halo_frame(f):
+        @pl.when(tm > 0)
+        def _():
+            x_next[f].wait_recv()
+            x_fwd[f].start()
+
+    def finish_frame(f):
         zed = column_sum(yacc[f], False) + bias[...]
         sig = jax.nn.sigmoid(zed)
         out_ref[0, f] = (zed * sig).astype(jnp.bfloat16).reshape(8, 32, 128)
         cot = cotv[f].reshape(256, 128).astype(jnp.float32)
         dz = (cot * sig * (1.0 + zed * (1.0 - sig))).astype(jnp.bfloat16)
         dzs[f, own] = dz.reshape(8, 32, 128)
-        bias_part += jnp.sum(dz.astype(jnp.float32).reshape(16, 16, 128), axis=0)
-
-    d_pair = remote(dzs.at[two, own], dzs.at[two, own], dsend.at[0], drecv.at[0], (dp, tm, other))
+        d_pair[f].start()
+        return jnp.sum(dz.astype(jnp.float32).reshape(16, 16, 128), axis=0)
+
+    d_pair = [
+        remote(dzs.at[f, own], dzs.at[f, own], dsend.at[3 * f], drecv.at[3 * f], (dp, tm, other))
+        for f in range(2)
+    ]
+
+    pl.when(tm > 0)(x_edge.wait_recv)
+    halo_frame(1)
+    yacc[0] += mm(scaled(x_rows(1), m1[0]), w_fwd(1))
+    yacc[1] += mm(scaled(x_rows(1), m0[1]), w_fwd(0))
+    bias_part = finish_frame(1)
+    halo_frame(0)
+    yacc[0] += mm(scaled(x_rows(0), m0[0]), w_fwd(0))
+    bias_part += finish_frame(0)
+
     d_next = remote(dzs.at[two, own], dzs.at[later, own], dsend.at[1], drecv.at[1], (dp, before, core))
     d_edge = remote(dzs.at[two, edge], dzs.at[later, edge], dsend.at[2], drecv.at[2], (dp, before, other))
-    d_pair.start()
-
-    @pl.when(zl > 0)
-    def _():
+
+    early = dp < zh_n // 2
+    near = zl > 0
+
+    def d_start():
         d_next.start()
         d_edge.start()
 
-    part[pl.ds(BIAS_ROW, 16), :] = bias_part.astype(jnp.bfloat16)
-    part[pl.ds(BIAS_ROW + 16, ROWS - BIAS_ROW - 16), :] = jnp.zeros((ROWS - BIAS_ROW - 16, 128), jnp.bfloat16)
-    pl.when(tm > 0)(x_fwd.wait_recv)
-    turned(0)
-    turned(1)
-    d_pair.wait_recv()
+    pl.when(near | (early & (tm > 0)))(d_start)
+
+    part[pl.ds(tile_row(p_n, 3, 0), 16), :] = bias_part.astype(jnp.bfloat16)
+    for spare in range(1, ROWS // 16 - 3 * TILES):
+        part[pl.ds(tile_row(p_n, 3, spare), 16), :] = jnp.zeros((16, 128), jnp.bfloat16)
+    for f in (1, 0):
+        pl.when(tm > 0)(x_fwd[f].wait_recv)
+        turned(f)
+    d_pair[1].wait_recv()
+    d_pair[0].wait_recv()
 
     right_side = jnp.concatenate(
         [
@@ -217,24 +260,33 @@
     def chunk_rows(q):
         return pl.ds(pl.multiple_of(q * chunk, 16), chunk)
 
-    def rs_start(q):
-        @pl.when(q != p)
-        def _():
-            slot = (p + p_n - q - 1) % p_n
-            remote(part.at[chunk_rows(q)], rsbuf.at[slot], rs_send, rs_recv, plane_dev(q)).start()
-
-    sent = 0
+    x_n = p_n // PLANE_Y
+    xq = [(p // PLANE_Y + dx) % x_n * PLANE_Y for dx in range(x_n)]
+    yq = [(p % PLANE_Y + dy) % PLANE_Y for dy in range(PLANE_Y)]
+    far_first = sorted(range(x_n), key=lambda dx: -min(dx, x_n - dx))
+
+    per = TILES // p_n * 16
     for k in range(3):
         grad = mm(lt[k], right_side)
         for a in range(3):
             for b in range(3):
-                tap = (k * 3 + a) * 3 + b
-                part[pl.ds(tap * HALF, HALF), :] = grad[
-                    b * HALF : (b + 1) * HALF, a * 128 : (a + 1) * 128
-                ].astype(jnp.bfloat16)
-        ready = p_n if k == 2 else (k + 1) * 9 * HALF // chunk
-        pl.loop(sent, ready)(rs_start)
-        sent = ready
+                for j in range(HALF // 16):
+                    block = grad[b * HALF + j * 16 : b * HALF + j * 16 + 16, a * 128 : (a + 1) * 128]
+                    row = tile_row(p_n, k, (a * 3 + b) * (HALF // 16) + j)
+                    part[pl.ds(row, 16), :] = block.astype(jnp.bfloat16)
+        count = per if k < 2 else chunk - 2 * per
+
+        for dx in far_first:
+            for dy in range(0 if dx else 1, PLANE_Y):
+                q = xq[dx] + yq[dy]
+                remote(
+                    part.at[pl.ds(pl.multiple_of(q * chunk + k * per, 16), count)],
+                    rsbuf.at[dx * PLANE_Y + dy - 1, pl.ds(k * per, count)], rs_send, rs_recv, plane_dev(q),
+                ).start()
+
+    hear(0)
+    if len(rounds) > 1:
+        tell(1)
 
     def d_rows(f):
         return jnp.concatenate(
@@ -253,6 +305,10 @@
     )
     yacc[1] = mm_t(d_rows(1), w_back(2))
 
+    for r in range(1, len(rounds) - 1):
+        hear(r)
+        tell(r + 1)
+
     remote(rsbuf, rsbuf, rs_send, rs_recv, plane_dev(p)).wait_recv()
     total = part[chunk_rows(p), :].astype(jnp.float32)
     for q in range(p_n - 1):
@@ -260,16 +316,20 @@
     zs[...] = total.astype(jnp.bfloat16)
 
     def owner_of(j):
-        return (z_n + j - owners // 2) % z_n
-
-    mine = (z + owners // 2) % z_n
+        return (z_n + j - (owners - 2)) % z_n
+
+    mine = (z + owners - 2) % z_n
     is_owner = mine < owners
 
     def zs_rows(j):
         return pl.ds(pl.multiple_of(j * piece, 16), piece)
 
+    if len(rounds) > 1:
+        hear(len(rounds) - 1)
+
     @pl.loop(0, owners)
-    def _(j):
+    def _(i):
+        j = owners - 1 - i
         w = owner_of(j)
 
         @pl.when(w != z)
@@ -277,13 +337,6 @@
             slot = (z + z_n - w - 1) % z_n
             remote(zs.at[zs_rows(j)], zbuf.at[slot], z_send, z_recv, z_dev(w)).start()
 
-    @pl.when(zl == 0)
-    def _():
-        @pl.when(tm > 0)
-        def _():
-            d_next.start()
-            d_edge.start()
-
     def piece_rows(owner, j):
         return pl.ds(pl.multiple_of(owner * chunk + j * piece, 16), piece)
 
@@ -295,11 +348,11 @@
     def pg_start(j):
         rows = piece_rows(p, j)
 
-        @pl.loop(1, p_n)
-        def _(i):
-            remote(
-                full.at[core, rows], full.at[core, rows], pg_send, pg_recv.at[p], plane_dev((p + i) % p_n)
-            ).start()
+        for dx in far_first:
+            @pl.loop(0 if dx else 1, PLANE_Y)
+            def _(dy):
+                q = xq[dx] + (p % PLANE_Y + dy) % PLANE_Y
+                remote(full.at[core, rows], full.at[core, rows], pg_send, pg_recv.at[p], plane_dev(q)).start()
 
     @pl.when(is_owner)
     def _():
@@ -315,29 +368,34 @@
 
         pg_start(mine)
 
-    for j in sorted(range(owners), key=lambda j: abs(j - owners // 2)):
+    for j in sorted(range(owners), key=lambda j: abs(j - (owners - 2))):
         @pl.when(owner_of(j) != z)
         def _():
             zg_copy(j, owner_of(j)).wait_recv()
             pg_start(j)
 
+    pl.when(jnp.logical_not(near | early) & (tm > 0))(d_start)
+
     def cg_copy(rows):
         return remote(full.at[core, rows], full.at[core, rows], cg_send, cg_recv, (dp, tm, other))
 
     cg_copy(chunk_rows(p)).start()
 
-    @pl.when(tm < tm_n - 1)
-    def _():
-        d_next.wait_recv()
-        d_edge.wait_recv()
-
-    yacc[0] += mm_t(scaled(d_rows(2), m0[2]), w_back(0))
-    yacc[1] += mm_t(
-        jnp.concatenate([scaled(d_rows(2), m1[2]), scaled(d_rows(3), m0[3])], axis=1),
-        jnp.concatenate([w_back(1), w_back(0)], axis=1),
-    )
-    for f in range(2):
-        ig_ref[0, f] = column_sum(yacc[f], True).astype(jnp.bfloat16).reshape(8, 32, 128)
+    def rest_of_in_grad():
+        @pl.when(tm < tm_n - 1)
+        def _():
+            d_next.wait_recv()
+            d_edge.wait_recv()
+
+        yacc[0] += mm_t(scaled(d_rows(2), m0[2]), w_back(0))
+        yacc[1] += mm_t(
+            jnp.concatenate([scaled(d_rows(2), m1[2]), scaled(d_rows(3), m0[3])], axis=1),
+            jnp.concatenate([w_back(1), w_back(0)], axis=1),
+        )
+        for f in range(2):
+            ig_ref[0, f] = column_sum(yacc[f], True).astype(jnp.bfloat16).reshape(8, 32, 128)
+
+    pl.when(early)(rest_of_in_grad)
 
     @pl.loop(1, p_n)
     def _(i):
@@ -346,17 +404,22 @@
         remote(full.at[core, rows], full.at[core, rows], pg_send, pg_recv.at[q], plane_dev(q)).wait_recv()
         cg_copy(rows).start()
 
+    pl.when(jnp.logical_not(early))(rest_of_in_grad)
+
     @pl.when(tm < tm_n - 1)
     def _():
-        x_next.wait_send()
+        x_next[0].wait_send()
+        x_next[1].wait_send()
         x_edge.wait_send()
 
     x_pair.wait_send()
-    d_pair.wait_send()
+    d_pair[0].wait_send()
+    d_pair[1].wait_send()
 
     @pl.when(tm > 0)
     def _():
-        x_fwd.wait_send()
+        x_fwd[0].wait_send()
+        x_fwd[1].wait_send()
         d_next.wait_send()
         d_edge.wait_send()
 
@@ -379,7 +442,7 @@
     everything.wait_recv()
 
 
-def finish_kernel(out_in, ig_in, full, out_ref, ig_ref, grad_ref, bias_ref, buf, bias_buf, sems):
+def finish_kernel(p_n, out_in, ig_in, full, out_ref, ig_ref, grad_ref, bias_ref, buf, bias_buf, sems):
     copies = [
         pltpu.make_async_copy(out_in, out_ref, sems.at[0]),
         pltpu.make_async_copy(ig_in, ig_ref, sems.at[1]),
@@ -387,21 +450,29 @@
     for k in range(3):
         for a in range(3):
             for b in range(3):
-                tap = (k * 3 + a) * 3 + b
                 for side in range(2):
-                    buf[k, a, b, pl.ds(side * HALF, HALF), :] = full[side, pl.ds(tap * HALF, HALF), :].astype(
-                        jnp.float32
-                    )
+                    for j in range(HALF // 16):
+                        row = tile_row(p_n, k, (a * 3 + b) * (HALF // 16) + j)
+                        buf[k, a, b, pl.ds(side * HALF + j * 16, 16), :] = full[
+                            side, pl.ds(row, 16), :
+                        ].astype(jnp.float32)
             copies.append(pltpu.make_async_copy(buf.at[k, a], grad_ref.at[k, a], sems.at[3 + 3 * k + a]))
             copies[-1].start()
     copies[0].start()
     copies[1].start()
-    terms = full[:, pl.ds(BIAS_ROW, 16), :].astype(jnp.float32)
+    terms = full[:, pl.ds(tile_row(p_n, 3, 0), 16), :].astype(jnp.float32)
     bias_buf[...] = jnp.sum(terms[0] + terms[1], axis=0, keepdims=True)
     copies.append(pltpu.make_async_copy(bias_buf, bias_ref, sems.at[2]))
     copies[-1].start()
     for copy in copies:
         copy.wait()
+
+
+def rounds_of(z_n):
+    rounds = [1]
+    while 2 * rounds[-1] < z_n // 2:
+        rounds.append(2 * rounds[-1])
+    return rounds
 
 
 def pieces(dims):
@@ -443,7 +514,8 @@
             pltpu.VMEM((p_n - 1, chunk, 128), jnp.bfloat16),
             pltpu.VMEM((chunk, 128), jnp.bfloat16),
             pltpu.VMEM((z_n - 1, piece, 128), jnp.bfloat16),
-            dma((5,)), dma((4,)), dma((4,)), dma((3,)), dma((3,)),
+            pltpu.SemaphoreType.REGULAR((len(rounds_of(z_n)),)),
+            dma((5,)), dma((6,)), dma((6,)), dma((4,)), dma((4,)),
             dma, dma, dma, dma, dma, dma((owners,)), dma, dma((p_n,)), dma, dma,
         ],
         compiler_params=pltpu.CompilerParams(
@@ -452,7 +524,7 @@
         name="chip_kernel",
     )(*(pltpu.with_memory_space_constraint(a, pltpu.HBM) for a in operands))
     result, in_grad, kern_grad, bias_grad = pl.pallas_call(
-        finish_kernel,
+        functools.partial(finish_kernel, p_n),
         out_shape=(
             jax.ShapeDtypeStruct(block, jnp.bfloat16),
             jax.ShapeDtypeStruct(block, jnp.bfloat16),

time: 56.1 us -> 53.8 us (0.959)
  Pallas kernels: 55.4 us -> 53 us
    pallas_call x1, Pallas kernels: 54 us -> 51.6 us  [on_device(): pl.pallas_call(functools.partial(chip_kernel, dims), out_shape=(jax.Shape...]
where the time goes in v3:
time: 53.8 us; the launch traced here: 53.6 us
  Pallas kernels  53 us (99%)
  between operations  0.64 us (1%)
    pallas_call x1, Pallas kernels, on_device(): pl.pallas_call(functools.partial(chip_kernel, dims), out_shape=(jax.Shape...  51.6 us
    pallas_call x1, Pallas kernels, on_device(): pl.pallas_call(functools.partial(finish_kernel, p_n), out_shape=(jax.Shap...  1.42 us

profile of v3, /device:TPU:1, one launch (start us, length us, event | category | flops | bytes accessed | tf_op | source)
XLA Modules:
  0.0 53.6 jit_solution(18369044838895850934)
XLA Ops:
  0.6 51.6 %chip_kernel.1 = (bf16[1,2,8,32,128]{4,3,2,1,0:T(8,128)(2,1)S(1)}, bf16[1,2,8,32,128]{4,3,2,1,0:T(8,128)(2,1)S(1)}, bf16[2,1792,128]{2,1,0:T(8,128)(2,1)S(1)}) custom-call(s32[1,4]{1,0:T(1,128)} %lens_hbm.1, bf16[1,2,8,32,128]{4,3,2,1,0:T(8,128)(2,1)} %x_hbm.1, bf16[3,3,3,128,128]{4,3,2,1,0:T(8,128)(2,1)} %w_hbm.1, f32[1,128]{1,0:T(1,128)} %bitcast.2, ...), custom_call_target="tpu_custom_call" | custom-call | tf_op jit(solution)/shard_map/chip_kernel/pallas_call | solution.py:494
  52.2 1.4 %finish_kernel.1 = (bf16[1,2,8,32,128]{4,3,2,1,0:T(8,128)(2,1)}, bf16[1,2,8,32,128]{4,3,2,1,0:T(8,128)(2,1)}, f32[3,3,3,128,128]{4,3,2,1,0:T(8,128)}, f32[1,128]{1,0:T(1,128)}) custom-call(bf16[1,2,8,32,128]{4,3,2,1,0:T(8,128)(2,1)S(1)} %get-tuple-element.11.out_in, bf16[1,2,8,32,128]{4,3,2,1,0:T(8,128)(2,1)S(1)} %get-tuple-element.12.ig_in, ...), custom_call_target="tpu_custom_call" | custom-call | tf_op jit(solution)/shard_map/finish_kernel/pallas_call | solution.py:526

commit v4 on v3

--- a/solution.py
+++ b/solution.py
@@ -50,12 +50,12 @@
     dims, lens_hbm, x_hbm, w_hbm, bias_hbm, cot_hbm,
     out_ref, ig_ref, full,
     lens, bias, xs, xt, lt, dzs, wv, cotv, yacc, part, rsbuf, zs, zbuf,
-    known, loc, xsend, xrecv, dsend, drecv, rs_send, rs_recv, z_send, z_recv,
+    known, plane_known, pair_ready, loc, xsend, xrecv, dsend, drecv, rs_send, rs_recv, z_send, z_recv,
     zg_send, zg_recv, pg_send, pg_recv, cg_send, cg_recv,
 ):
     zh_n, tm_n = dims
     z_n, p_n = zh_n * Z_LO, tm_n // Z_LO
-    chunk, piece, owners = pieces(dims)
+    chunk = ROWS // p_n
     rounds = rounds_of(z_n)
 
     dp, tm, core = lax.axis_index("dp"), lax.axis_index("tm"), lax.axis_index("space")
@@ -69,6 +69,16 @@
 
     def z_dev(w):
         return (w // Z_LO, p * Z_LO + w % Z_LO, core)
+
+    x_n = p_n // PLANE_Y
+    xq = [(p // PLANE_Y + dx) % x_n * PLANE_Y for dx in range(x_n)]
+    yq = [(p % PLANE_Y + dy) % PLANE_Y for dy in range(PLANE_Y)]
+    far_first = sorted(
+        ((dx, dy) for dx in range(x_n) for dy in range(PLANE_Y) if dx + dy),
+        key=lambda d: -min(d[0], x_n - d[0]) - min(d[1], PLANE_Y - d[1]),
+    )
+    next_to = [xq[dx] + yq[0] for dx in (1, x_n - 1) if x_n > 1] + [xq[0] + yq[dy] for dy in (1, PLANE_Y - 1)]
+    two_off = [xq[dx] + yq[0] for dx in range(2, x_n, x_n)] + [xq[0] + yq[dy] for dy in range(2, PLANE_Y, PLANE_Y)]
 
     barrier = pltpu.get_barrier_semaphore()
 
@@ -93,7 +103,8 @@
             greet((dp, near, core))
             greet((dp, near, other))
 
-    pl.loop(1, p_n)(lambda i: greet(plane_dev((p + i) % p_n)))
+    for q in next_to:
+        greet(plane_dev(q))
     greet(z_dev((z + 1) % z_n))
     greet(z_dev((z + z_n - 1) % z_n))
 
@@ -127,7 +138,15 @@
 
     get_x.wait()
     sides = (tm + tm_n - 1) // tm_n + (2 * (tm_n - 1) - tm) // tm_n
-    pl.semaphore_wait(barrier, 1 + (p_n - 1) + 2 + 2 * sides)
+    pl.semaphore_wait(barrier, 1 + len(next_to) + 2 + 2 * sides)
+
+    def tell_plane(r):
+        for q in (next_to, two_off)[r]:
+            pl.semaphore_signal(plane_known.at[r], inc=1, device_id=plane_dev(q), device_id_type=MESH)
+
+    def hear_plane(r):
+        if (next_to, two_off)[r]:
+            pl.semaphore_wait(plane_known.at[r], len((next_to, two_off)[r]))
 
     def tell(r):
         for w in (z + rounds[r], z + z_n - rounds[r]):
@@ -136,6 +155,7 @@
     def hear(r):
         pl.semaphore_wait(known.at[r], 2)
 
+    tell_plane(0)
     tell(0)
 
     x_next = [
@@ -219,6 +239,8 @@
         for f in range(2)
     ]
 
+    hear_plane(0)
+    tell_plane(1)
     pl.when(tm > 0)(x_edge.wait_recv)
     halo_frame(1)
     yacc[0] += mm(scaled(x_rows(1), m1[0]), w_fwd(1))
@@ -231,7 +253,7 @@
     d_next = remote(dzs.at[two, own], dzs.at[later, own], dsend.at[1], drecv.at[1], (dp, before, core))
     d_edge = remote(dzs.at[two, edge], dzs.at[later, edge], dsend.at[2], drecv.at[2], (dp, before, other))
 
-    early = dp < zh_n // 2
+    early, middle = dp < zh_n // 2, dp == zh_n // 2
     near = zl > 0
 
     def d_start():
@@ -259,11 +281,6 @@
 
     def chunk_rows(q):
         return pl.ds(pl.multiple_of(q * chunk, 16), chunk)
-
-    x_n = p_n // PLANE_Y
-    xq = [(p // PLANE_Y + dx) % x_n * PLANE_Y for dx in range(x_n)]
-    yq = [(p % PLANE_Y + dy) % PLANE_Y for dy in range(PLANE_Y)]
-    far_first = sorted(range(x_n), key=lambda dx: -min(dx, x_n - dx))
 
     per = TILES // p_n * 16
     for k in range(3):
@@ -275,14 +292,15 @@
                     row = tile_row(p_n, k, (a * 3 + b) * (HALF // 16) + j)
                     part[pl.ds(row, 16), :] = block.astype(jnp.bfloat16)
         count = per if k < 2 else chunk - 2 * per
-
-        for dx in far_first:
-            for dy in range(0 if dx else 1, PLANE_Y):
-                q = xq[dx] + yq[dy]
-                remote(
-                    part.at[pl.ds(pl.multiple_of(q * chunk + k * per, 16), count)],
-                    rsbuf.at[dx * PLANE_Y + dy - 1, pl.ds(k * per, count)], rs_send, rs_recv, plane_dev(q),
-                ).start()
+        if k == 0:
+            hear_plane(1)
+
+        for dx, dy in far_first:
+            q = xq[dx] + yq[dy]
+            remote(
+                part.at[pl.ds(pl.multiple_of(q * chunk + k * per, 16), count)],
+                rsbuf.at[dx * PLANE_Y + dy - 1, pl.ds(k * per, count)], rs_send, rs_recv, plane_dev(q),
+            ).start()
 
     hear(0)
     if len(rounds) > 1:
@@ -315,71 +333,12 @@
         total += rsbuf[q].astype(jnp.float32)
     zs[...] = total.astype(jnp.bfloat16)
 
-    def owner_of(j):
-        return (z_n + j - (owners - 2)) % z_n
-
-    mine = (z + owners - 2) % z_n
-    is_owner = mine < owners
-
-    def zs_rows(j):
-        return pl.ds(pl.multiple_of(j * piece, 16), piece)
-
     if len(rounds) > 1:
         hear(len(rounds) - 1)
 
-    @pl.loop(0, owners)
-    def _(i):
-        j = owners - 1 - i
-        w = owner_of(j)
-
-        @pl.when(w != z)
-        def _():
-            slot = (z + z_n - w - 1) % z_n
-            remote(zs.at[zs_rows(j)], zbuf.at[slot], z_send, z_recv, z_dev(w)).start()
-
-    def piece_rows(owner, j):
-        return pl.ds(pl.multiple_of(owner * chunk + j * piece, 16), piece)
-
-    def zg_copy(j, w):
-        return remote(
-            full.at[core, piece_rows(p, j)], full.at[core, piece_rows(p, j)], zg_send, zg_recv.at[j], z_dev(w)
-        )
-
-    def pg_start(j):
-        rows = piece_rows(p, j)
-
-        for dx in far_first:
-            @pl.loop(0 if dx else 1, PLANE_Y)
-            def _(dy):
-                q = xq[dx] + (p % PLANE_Y + dy) % PLANE_Y
-                remote(full.at[core, rows], full.at[core, rows], pg_send, pg_recv.at[p], plane_dev(q)).start()
-
-    @pl.when(is_owner)
-    def _():
-        remote(zbuf, zbuf, z_send, z_recv, z_dev(z)).wait_recv()
-        acc = zs[zs_rows(mine), :].astype(jnp.float32)
-        for w in range(z_n - 1):
-            acc += zbuf[w].astype(jnp.float32)
-        full[core, piece_rows(p, mine)] = acc.astype(jnp.bfloat16)
-
-        @pl.loop(0, z_n)
-        def _(w):
-            pl.when(w != z)(lambda: zg_copy(mine, w).start())
-
-        pg_start(mine)
-
-    for j in sorted(range(owners), key=lambda j: abs(j - (owners - 2))):
-        @pl.when(owner_of(j) != z)
-        def _():
-            zg_copy(j, owner_of(j)).wait_recv()
-            pg_start(j)
-
-    pl.when(jnp.logical_not(near | early) & (tm > 0))(d_start)
-
-    def cg_copy(rows):
-        return remote(full.at[core, rows], full.at[core, rows], cg_send, cg_recv, (dp, tm, other))
-
-    cg_copy(chunk_rows(p)).start()
+    to_first = remote(zs, zbuf.at[(z + z_n - 1) % z_n], z_send, z_recv, z_dev(z * 0))
+    pl.when(z > 0)(to_first.start)
+    pl.when(jnp.logical_not(near) & middle & (tm > 0))(d_start)
 
     def rest_of_in_grad():
         @pl.when(tm < tm_n - 1)
@@ -395,7 +354,47 @@
         for f in range(2):
             ig_ref[0, f] = column_sum(yacc[f], True).astype(jnp.bfloat16).reshape(8, 32, 128)
 
-    pl.when(early)(rest_of_in_grad)
+    pl.when(early | middle)(rest_of_in_grad)
+
+    half = z_n // 2
+    mine = full.at[core, chunk_rows(p)]
+
+    def z_share(w):
+        remote(mine, mine, zg_send, zg_recv, z_dev(w)).start()
+
+    @pl.when(z == 0)
+    def _():
+        remote(zbuf, zbuf, z_send, z_recv, z_dev(z)).wait_recv()
+        acc = zs[...].astype(jnp.float32)
+        for w in range(z_n - 1):
+            acc += zbuf[w].astype(jnp.float32)
+        full[core, chunk_rows(p), :] = acc.astype(jnp.bfloat16)
+        for w in range(1, min(4, half)):
+            z_share(w)
+        pl.semaphore_signal(pair_ready, inc=1, device_id=(dp, tm, other), device_id_type=MESH)
+
+    pl.when(z > 0)(lambda: remote(mine, mine, zg_send, zg_recv, z_dev(z)).wait_recv())
+
+    @pl.when(z == z_n - 1)
+    def _():
+        for w in range(half, z_n - 1):
+            z_share(w)
+
+    for dx, dy in far_first:
+        remote(mine, mine, pg_send, pg_recv.at[p], plane_dev(xq[dx] + yq[dy])).start()
+
+    @pl.when(z == 0)
+    def _():
+        pl.semaphore_wait(pair_ready, 1)
+        for w in (*range(4, half), z_n - 1):
+            z_share(w)
+
+    pl.when(jnp.logical_not(near | early | middle) & (tm > 0))(d_start)
+
+    def cg_copy(rows):
+        return remote(full.at[core, rows], full.at[core, rows], cg_send, cg_recv, (dp, tm, other))
+
+    cg_copy(chunk_rows(p)).start()
 
     @pl.loop(1, p_n)
     def _(i):
@@ -404,7 +403,7 @@
         remote(full.at[core, rows], full.at[core, rows], pg_send, pg_recv.at[q], plane_dev(q)).wait_recv()
         cg_copy(rows).start()
 
-    pl.when(jnp.logical_not(early))(rest_of_in_grad)
+    pl.when(jnp.logical_not(early | middle))(rest_of_in_grad)
 
     @pl.when(tm < tm_n - 1)
     def _():
@@ -426,15 +425,11 @@
     rest = pl.ds(0, (p_n - 1) * chunk)
     remote(part.at[rest], part.at[rest], rs_send, rs_recv, plane_dev(p)).wait_send()
 
-    @pl.when(is_owner)
-    def _():
-        most = zs.at[pl.ds(0, (owners - 1) * piece)]
-        remote(most, most, z_send, z_recv, z_dev(z)).wait_send()
-        remote(zbuf, zbuf, zg_send, z_recv, z_dev(z)).wait_send()
-
-    @pl.when(jnp.logical_not(is_owner))
-    def _():
-        remote(zs, zs, z_send, z_recv, z_dev(z)).wait_send()
+    pl.when(z > 0)(to_first.wait_send)
+    for w, count in ((0, half), (z_n - 1, half - 1)):
+        if count:
+            sent = zbuf.at[pl.ds(0, count)]
+            pl.when(z == w)(remote(sent, sent, zg_send, z_recv, z_dev(z)).wait_send)
 
     remote(full.at[core, rest], full.at[core, rest], pg_send, pg_recv.at[p], plane_dev(p)).wait_send()
     everything = remote(full.at[core], full.at[other], cg_send, cg_recv, (dp, tm, other))
@@ -475,18 +470,10 @@
     return rounds
 
 
-def pieces(dims):
+def on_device(dims, inputs, clip_lengths, weight, bias, cotangent):
     zh_n, tm_n = dims
     z_n, p_n = zh_n * Z_LO, tm_n // Z_LO
     chunk = ROWS // p_n
-    piece = 16 * max(1, chunk // 16 // z_n)
-    return chunk, piece, chunk // piece
-
-
-def on_device(dims, inputs, clip_lengths, weight, bias, cotangent):
-    zh_n, tm_n = dims
-    z_n, p_n = zh_n * Z_LO, tm_n // Z_LO
-    chunk, piece, owners = pieces(dims)
     block = inputs.shape
     dma = pltpu.SemaphoreType.DMA
     vmem, hbm = (pl.BlockSpec(memory_space=m) for m in (pltpu.VMEM, pltpu.HBM))
@@ -513,10 +500,12 @@
             pltpu.VMEM((ROWS, 128), jnp.bfloat16),
             pltpu.VMEM((p_n - 1, chunk, 128), jnp.bfloat16),
             pltpu.VMEM((chunk, 128), jnp.bfloat16),
-            pltpu.VMEM((z_n - 1, piece, 128), jnp.bfloat16),
+            pltpu.VMEM((z_n - 1, chunk, 128), jnp.bfloat16),
             pltpu.SemaphoreType.REGULAR((len(rounds_of(z_n)),)),
+            pltpu.SemaphoreType.REGULAR((2,)),
+            pltpu.SemaphoreType.REGULAR,
             dma((5,)), dma((6,)), dma((6,)), dma((4,)), dma((4,)),
-            dma, dma, dma, dma, dma, dma((owners,)), dma, dma((p_n,)), dma, dma,
+            dma, dma, dma, dma, dma, dma, dma, dma((p_n,)), dma, dma,
         ],
         compiler_params=pltpu.CompilerParams(
             collective_id=0, has_side_effects=True, vmem_limit_bytes=40 * 1024 * 1024

time: 53.8 us -> 51 us (0.948)
  the two profiles are of different devices: /device:TPU:1 before, /device:TPU:225 now
where the time goes in v4:
time: 51 us; the launch traced here: 50.9 us
  Pallas kernels  50.3 us (99%)
  between operations  0.64 us (1%)
    pallas_call x1, Pallas kernels, on_device(): pl.pallas_call(functools.partial(chip_kernel, dims), out_shape=(jax.Shape...  48.8 us
    pallas_call x1, Pallas kernels, on_device(): pl.pallas_call(functools.partial(finish_kernel, p_n), out_shape=(jax.Shap...  1.42 us

profile of v4, /device:TPU:225, one launch (start us, length us, event | category | flops | bytes accessed | tf_op | source)
XLA Modules:
  0.0 50.9 jit_solution(4613360524602379935)
XLA Ops:
  0.6 48.8 %chip_kernel.1 = (bf16[1,2,8,32,128]{4,3,2,1,0:T(8,128)(2,1)S(1)}, bf16[1,2,8,32,128]{4,3,2,1,0:T(8,128)(2,1)S(1)}, bf16[2,1792,128]{2,1,0:T(8,128)(2,1)S(1)}) custom-call(s32[1,4]{1,0:T(1,128)} %lens_hbm.1, bf16[1,2,8,32,128]{4,3,2,1,0:T(8,128)(2,1)} %x_hbm.1, bf16[3,3,3,128,128]{4,3,2,1,0:T(8,128)(2,1)} %w_hbm.1, f32[1,128]{1,0:T(1,128)} %bitcast.2, ...), custom_call_target="tpu_custom_call" | custom-call | tf_op jit(solution)/shard_map/chip_kernel/pallas_call | solution.py:481
  49.5 1.4 %finish_kernel.1 = (bf16[1,2,8,32,128]{4,3,2,1,0:T(8,128)(2,1)}, bf16[1,2,8,32,128]{4,3,2,1,0:T(8,128)(2,1)}, f32[3,3,3,128,128]{4,3,2,1,0:T(8,128)}, f32[1,128]{1,0:T(1,128)}) custom-call(bf16[1,2,8,32,128]{4,3,2,1,0:T(8,128)(2,1)S(1)} %get-tuple-element.11.out_in, bf16[1,2,8,32,128]{4,3,2,1,0:T(8,128)(2,1)S(1)} %get-tuple-element.12.ig_in, ...), custom_call_target="tpu_custom_call" | custom-call | tf_op jit(solution)/shard_map/finish_kernel/pallas_call | solution.py:515

commit v5 on v4

--- a/solution.py
+++ b/solution.py
@@ -50,7 +50,7 @@
     dims, lens_hbm, x_hbm, w_hbm, bias_hbm, cot_hbm,
     out_ref, ig_ref, full,
     lens, bias, xs, xt, lt, dzs, wv, cotv, yacc, part, rsbuf, zs, zbuf,
-    known, plane_known, pair_ready, loc, xsend, xrecv, dsend, drecv, rs_send, rs_recv, z_send, z_recv,
+    known, plane_known, loc, xsend, xrecv, dsend, drecv, rs_send, rs_recv, z_send, z_recv,
     zg_send, zg_recv, pg_send, pg_recv, cg_send, cg_recv,
 ):
     zh_n, tm_n = dims
@@ -369,9 +369,8 @@
         for w in range(z_n - 1):
             acc += zbuf[w].astype(jnp.float32)
         full[core, chunk_rows(p), :] = acc.astype(jnp.bfloat16)
-        for w in range(1, min(4, half)):
+        for w in (*range(1, half), z_n - 1):
             z_share(w)
-        pl.semaphore_signal(pair_ready, inc=1, device_id=(dp, tm, other), device_id_type=MESH)
 
     pl.when(z > 0)(lambda: remote(mine, mine, zg_send, zg_recv, z_dev(z)).wait_recv())
 
@@ -383,11 +382,6 @@
     for dx, dy in far_first:
         remote(mine, mine, pg_send, pg_recv.at[p], plane_dev(xq[dx] + yq[dy])).start()
 
-    @pl.when(z == 0)
-    def _():
-        pl.semaphore_wait(pair_ready, 1)
-        for w in (*range(4, half), z_n - 1):
-            z_share(w)
 
     pl.when(jnp.logical_not(near | early | middle) & (tm > 0))(d_start)
 
@@ -503,7 +497,6 @@
             pltpu.VMEM((z_n - 1, chunk, 128), jnp.bfloat16),
             pltpu.SemaphoreType.REGULAR((len(rounds_of(z_n)),)),
             pltpu.SemaphoreType.REGULAR((2,)),
-            pltpu.SemaphoreType.REGULAR,
             dma((5,)), dma((6,)), dma((6,)), dma((4,)), dma((4,)),
             dma, dma, dma, dma, dma, dma, dma, dma((p_n,)), dma, dma,
         ],

time: 51 us -> 50.7 us (level)
  the two profiles are of different devices: /device:TPU:225 before, /device:TPU:1 now
where the time goes in v5:
time: 50.7 us; the launch traced here: 50 us
  Pallas kernels  49.3 us (97%)
  between operations  0.64 us (1%)
    pallas_call x1, Pallas kernels, on_device(): pl.pallas_call(functools.partial(chip_kernel, dims), out_shape=(jax.Shape...  47.9 us
    pallas_call x1, Pallas kernels, on_device(): pl.pallas_call(functools.partial(finish_kernel, p_n), out_shape=(jax.Shap...  1.42 us

profile of v5, /device:TPU:1, one launch (start us, length us, event | category | flops | bytes accessed | tf_op | source)
XLA Modules:
  0.0 50.0 jit_solution(5985778992936980243)
XLA Ops:
  0.6 47.9 %chip_kernel.1 = (bf16[1,2,8,32,128]{4,3,2,1,0:T(8,128)(2,1)S(1)}, bf16[1,2,8,32,128]{4,3,2,1,0:T(8,128)(2,1)S(1)}, bf16[2,1792,128]{2,1,0:T(8,128)(2,1)S(1)}) custom-call(s32[1,4]{1,0:T(1,128)} %lens_hbm.1, bf16[1,2,8,32,128]{4,3,2,1,0:T(8,128)(2,1)} %x_hbm.1, bf16[3,3,3,128,128]{4,3,2,1,0:T(8,128)(2,1)} %w_hbm.1, f32[1,128]{1,0:T(1,128)} %bitcast.2, ...), custom_call_target="tpu_custom_call" | custom-call | tf_op jit(solution)/shard_map/chip_kernel/pallas_call | solution.py:475
  48.6 1.4 %finish_kernel.1 = (bf16[1,2,8,32,128]{4,3,2,1,0:T(8,128)(2,1)}, bf16[1,2,8,32,128]{4,3,2,1,0:T(8,128)(2,1)}, f32[3,3,3,128,128]{4,3,2,1,0:T(8,128)}, f32[1,128]{1,0:T(1,128)}) custom-call(bf16[1,2,8,32,128]{4,3,2,1,0:T(8,128)(2,1)S(1)} %get-tuple-element.11.out_in, bf16[1,2,8,32,128]{4,3,2,1,0:T(8,128)(2,1)S(1)} %get-tuple-element.12.ig_in, ...), custom_call_target="tpu_custom_call" | custom-call | tf_op jit(solution)/shard_map/finish_kernel/pallas_call | solution.py:508

commit v6 on v5

--- a/solution.py
+++ b/solution.py
@@ -364,7 +364,8 @@
 
     @pl.when(z == 0)
     def _():
-        remote(zbuf, zbuf, z_send, z_recv, z_dev(z)).wait_recv()
+        shares = zbuf.at[pl.ds(0, z_n - 1)]
+        remote(shares, shares, z_send, z_recv, z_dev(z)).wait_recv()
         acc = zs[...].astype(jnp.float32)
         for w in range(z_n - 1):
             acc += zbuf[w].astype(jnp.float32)
@@ -494,7 +495,7 @@
             pltpu.VMEM((ROWS, 128), jnp.bfloat16),
             pltpu.VMEM((p_n - 1, chunk, 128), jnp.bfloat16),
             pltpu.VMEM((chunk, 128), jnp.bfloat16),
-            pltpu.VMEM((z_n - 1, chunk, 128), jnp.bfloat16),
+            pltpu.VMEM((z_n, chunk, 128), jnp.bfloat16),
             pltpu.SemaphoreType.REGULAR((len(rounds_of(z_n)),)),
             pltpu.SemaphoreType.REGULAR((2,)),
             dma((5,)), dma((6,)), dma((6,)), dma((4,)), dma((4,)),

time: 50.7 us -> 50.7 us (level)
  no operation moved by 1% of the time
where the time goes in v6:
time: 50.7 us; the launch traced here: 50 us
  Pallas kernels  49.3 us (97%)
  between operations  0.64 us (1%)
    pallas_call x1, Pallas kernels, on_device(): pl.pallas_call(functools.partial(chip_kernel, dims), out_shape=(jax.Shape...  47.9 us
    pallas_call x1, Pallas kernels, on_device(): pl.pallas_call(functools.partial(finish_kernel, p_n), out_shape=(jax.Shap...  1.42 us

profile of v6, /device:TPU:1, one launch (start us, length us, event | category | flops | bytes accessed | tf_op | source)
XLA Modules:
  0.0 50.0 jit_solution(10751924684906587893)
XLA Ops:
  0.6 47.9 %chip_kernel.1 = (bf16[1,2,8,32,128]{4,3,2,1,0:T(8,128)(2,1)S(1)}, bf16[1,2,8,32,128]{4,3,2,1,0:T(8,128)(2,1)S(1)}, bf16[2,1792,128]{2,1,0:T(8,128)(2,1)S(1)}) custom-call(s32[1,4]{1,0:T(1,128)} %lens_hbm.1, bf16[1,2,8,32,128]{4,3,2,1,0:T(8,128)(2,1)} %x_hbm.1, bf16[3,3,3,128,128]{4,3,2,1,0:T(8,128)(2,1)} %w_hbm.1, f32[1,128]{1,0:T(1,128)} %bitcast.2, ...), custom_call_target="tpu_custom_call" | custom-call | tf_op jit(solution)/shard_map/chip_kernel/pallas_call | solution.py:476
  48.6 1.4 %finish_kernel.1 = (bf16[1,2,8,32,128]{4,3,2,1,0:T(8,128)(2,1)}, bf16[1,2,8,32,128]{4,3,2,1,0:T(8,128)(2,1)}, f32[3,3,3,128,128]{4,3,2,1,0:T(8,128)}, f32[1,128]{1,0:T(1,128)}) custom-call(bf16[1,2,8,32,128]{4,3,2,1,0:T(8,128)(2,1)S(1)} %get-tuple-element.11.out_in, bf16[1,2,8,32,128]{4,3,2,1,0:T(8,128)(2,1)S(1)} %get-tuple-element.12.ig_in, ...), custom_call_target="tpu_custom_call" | custom-call | tf_op jit(solution)/shard_map/finish_kernel/pallas_call | solution.py:509
